TPU v7x, 32 devices: a whole 2x2x4 slice. The times are simulated.
32 devices in a mesh: owner: 8 (over z, x), view: 4 (over y, core).
Axes of the slice: x: 2, y: 2, z: 4, core: 2. Of those that a mesh axis runs over, the one named last changes fastest.
Arguments:
- estimate: float32 [128, 128, 128], P('owner'), may hold values from 0.5 to 2
- axial_views: float32 [4, 128, 128, 128], P('view', 'owner'), may hold values from 0.3 to 3
- lateral_views: float32 [4, 128, 128, 128], P('view', 'owner'), may hold values from 0.3 to 3
- psf_axial: float32 [4, 3, 33], P('view'), may hold values from 0.05 to 1
- psf_lateral: float32 [4, 3, 33], P('view'), may hold values from 0.05 to 1
- coverage: int32 [8, 4, 8], P('owner'), may hold values from 0 to 1, as said below
Outputs:
- deconvolved: float32 [128, 128, 128], P('owner')
Inputs may be any that keep to these rules, and one draw needn't show every extreme that they name: `coverage`: each block is covered by 2 to 6 views; some block by exactly 6 and some by exactly 2.
All inputs are finite; a program needn't handle non-finite values.
Results may differ from a plain program's by a relative error of at most 0.0001.
Values sent between devices are 32-bit elements; how exact they have to be, the bound alone decides.
A program may use at most 128 MiB of HBM per device.

v0:
```python
import jax
import jax.numpy as jnp
from jax import lax
from jax.sharding import PartitionSpec as P

VA = 4
ITERS = 2


PRECISE = lax.Precision.HIGHEST


def extended(shard, sides, width):
    for axis, dim in sides:
        peers, length = (lax.axis_size(axis), shard.shape[dim])
        up = [(i, (i + 1) % peers) for i in range(peers - 1)]
        down = [(j, i) for i, j in up]
        last = lax.slice_in_dim(shard, length - width, length, axis=dim)
        leading = lax.slice_in_dim(shard, 0, width, axis=dim)
        before = lax.ppermute(last, axis, up)
        after = lax.ppermute(leading, axis, down)
        shard = jnp.concatenate([before, shard, after], axis=dim)
    return shard


def band_matrix(kernel, block_width):
    rim_width = (kernel.shape[-1] - 1) // 2
    row_index = jnp.arange(block_width + 2 * rim_width)[:, None]
    col_index = jnp.arange(block_width)[None, :]
    matches = (row_index - col_index)[:, :, None] == jnp.arange(kernel.shape[-1])[None, None, :]
    return jnp.sum(jnp.where(matches[None], kernel[:, None, None, :], 0.0), axis=-1)


def middle_matrix(kernel, length):
    rim_width = (kernel.shape[-1] - 1) // 2
    row_index = jnp.arange(length)[:, None]
    col_index = jnp.arange(length)[None, :]
    matches = (row_index - col_index + rim_width)[:, :, None] == jnp.arange(kernel.shape[-1])[
        None, None, :
    ]
    return jnp.sum(jnp.where(matches[None], kernel[:, None, None, :], 0.0), axis=-1)


def along_last(volume, kernel):
    rim_width = (kernel.shape[-1] - 1) // 2
    length = volume.shape[-1]
    block_width = min(128, length)
    blocks = volume.reshape(volume.shape[:-1] + (length // block_width, block_width))
    zero_rim = jnp.zeros(blocks.shape[:-2] + (1, rim_width), volume.dtype)
    left_rim = jnp.concatenate([zero_rim, blocks[..., :-1, block_width - rim_width :]], axis=-2)
    right_rim = jnp.concatenate([blocks[..., 1:, :rim_width], zero_rim], axis=-2)
    windows = jnp.concatenate([left_rim, blocks, right_rim], axis=-1)
    result = jnp.einsum(
        "vabns,vsi->vabni", windows, band_matrix(kernel, block_width), precision=PRECISE
    )
    return result.reshape(volume.shape)


def forward(padded, kernel_first, kernel_mid, kernel_last):
    plane_count = padded.shape[0] - (kernel_first.shape[-1] - 1)
    result = jnp.einsum(
        "syl,vsi->viyl", padded, band_matrix(kernel_first, plane_count), precision=PRECISE
    )
    result = jnp.einsum(
        "viyl,vyk->vikl", result, middle_matrix(kernel_mid, result.shape[2]), precision=PRECISE
    )
    return along_last(result, kernel_last)


def backward(padded, kernel_first, kernel_mid, kernel_last):
    plane_count = padded.shape[1] - (kernel_first.shape[-1] - 1)
    result = jnp.einsum(
        "vsyl,vsi->viyl", padded, band_matrix(kernel_first, plane_count), precision=PRECISE
    )
    result = jnp.einsum(
        "viyl,vyk->vikl", result, middle_matrix(kernel_mid, result.shape[2]), precision=PRECISE
    )
    return along_last(result, kernel_last)


def edge_weights(kernel, positions, length):
    rim_width = (kernel.shape[-1] - 1) // 2
    source = positions[:, None] + jnp.arange(kernel.shape[-1])[None, :] - rim_width
    inside = (source >= 0) & (source < length)
    return jnp.sum(jnp.where(inside[None], kernel[:, None, :], 0.0), axis=-1)


def log_correction(padded, kernel_first, kernel_mid, kernel_last, first_start, first_total):
    back_sum = backward(padded, kernel_first, kernel_mid, kernel_last)
    plane_count, line_count, column_count = back_sum.shape[1:]
    first_weights = edge_weights(kernel_first, first_start + jnp.arange(plane_count), first_total)
    mid_weights = edge_weights(kernel_mid, jnp.arange(line_count), line_count)
    last_weights = edge_weights(kernel_last, jnp.arange(column_count), column_count)
    scale_sum = (
        first_weights[:, :, None, None]
        * mid_weights[:, None, :, None]
        * last_weights[:, None, None, :]
    )
    return jnp.log(back_sum / scale_sum)


def select_views(covered, view_ids):
    picked = (jnp.arange(covered.shape[-1])[None, :] == view_ids[:, None]).astype(jnp.float32)
    return jnp.einsum("vw,xw->vx", picked, covered, precision=PRECISE)


def slab_logs(padded_estimate, view_data, kernel, flipped, weights, first_start, first_total):
    blurred = forward(padded_estimate, kernel[:, 0], kernel[:, 1], kernel[:, 2])
    quotient = view_data / blurred
    rim_width = (kernel.shape[-1] - 1) // 2
    quotient_padded = extended(quotient, (("owner", 1),), rim_width)
    log_terms = log_correction(
        quotient_padded, flipped[:, 0], flipped[:, 1], flipped[:, 2], first_start, first_total
    )
    return jnp.sum(weights[:, None, None, :] * log_terms, axis=0)


def local(estimate, axial_views, lateral_views, psf_axial, psf_lateral, coverage):
    plane_count, line_count, column_count = estimate.shape
    owners = lax.axis_size("owner")
    slab_index = lax.axis_index("owner")
    view_index = lax.axis_index("view")
    slab_width = column_count // owners
    rim_width = (psf_axial.shape[-1] - 1) // 2
    kernel_axial = psf_axial / jnp.sum(psf_axial, axis=-1, keepdims=True)
    kernel_lateral = psf_lateral / jnp.sum(psf_lateral, axis=-1, keepdims=True)
    flipped_axial = kernel_axial[..., ::-1]
    flipped_lateral = kernel_lateral[..., ::-1]
    block_width = column_count // coverage.shape[1]
    covered = jnp.repeat(coverage[0].astype(jnp.float32), block_width, axis=0)
    cover_count = jnp.sum(covered, axis=-1)
    axial_count = psf_axial.shape[0]
    lateral_count = psf_lateral.shape[0]
    weights_axial = select_views(covered, view_index * axial_count + jnp.arange(axial_count))
    weights_lateral = select_views(
        covered, VA + view_index * lateral_count + jnp.arange(lateral_count)
    )
    plane_start = slab_index * plane_count
    plane_total = plane_count * owners
    moved_views = lateral_views.reshape(
        lateral_count, slab_width, line_count, owners, plane_count
    ).transpose(0, 4, 2, 3, 1)
    lateral_slabs = lax.all_to_all(moved_views, "owner", split_axis=3, concat_axis=4, tiled=True)
    lateral_slabs = lateral_slabs.reshape(lateral_count, plane_count, line_count, column_count)
    view_all = jnp.concatenate([axial_views, lateral_slabs], axis=0)
    kernel_all = jnp.concatenate([kernel_axial, kernel_lateral], axis=0)
    flipped_all = jnp.concatenate([flipped_axial, flipped_lateral], axis=0)
    weights_all = jnp.concatenate([weights_axial, weights_lateral], axis=0)
    for iteration in range(ITERS):
        padded_estimate = extended(estimate, (("owner", 0),), rim_width)
        log_total = slab_logs(
            padded_estimate,
            view_all,
            kernel_all,
            flipped_all,
            weights_all,
            plane_start,
            plane_total,
        )
        log_total = lax.psum(log_total, "view")
        estimate = estimate * jnp.exp(log_total / cover_count[None, None, :])
    return estimate


def solution(mesh):
    in_specs = (
        P("owner", None, None),
        P("view", "owner", None, None),
        P("view", "owner", None, None),
        P("view", None, None),
        P("view", None, None),
        P("owner", None, None),
    )
    out_specs = P("owner", None, None)
    return jax.shard_map(local, mesh=mesh, in_specs=in_specs, out_specs=out_specs, check_vma=False)
```

profile of v0, /device:TPU:0, one launch (start us, length us, event | category | flops | bytes accessed | tf_op | source)
XLA Modules:
  0.0 474.0 jit_solution(12816885927386915285)
XLA Ops:
  9.7 6.5 %collective-permute-start = (f32[16,128,128]{2,0,1:T(8,128)S(1)}, f32[16,128,128]{2,0,1:T(8,128)}, u32[]{:S(2)}, u32[]{:S(2)}) collective-permute-start(f32[16,128,128]{2,0,1:T(8,128)S(1)} %copy.56), channel_id=1, source_target_pairs={{0,4},{4,8},{8,12},{12,16},{16,20},{20,24},{24,28},{1,5},{5,9},{9,... | collective-permute-start | bytes 3145736 | tf_op jit(solution)/shard_map/ppermute | solution.py:20
  18.8 5.2 %all-to-all-start = ((f32[1,16,128,8,16]{2,1,4,0,3:T(8,128)}), f32[1,16,128,8,16]{2,1,4,0,3:T(8,128)}, u32[]{:S(2)}, u32[]{:S(2)}) async-start(f32[1,16,128,8,16]{2,1,4,0,3:T(8,128)} %copy.44), calls=%async_computation | async-start | bytes 2097152 | tf_op jit(solution)/shard_map/all_to_all | solution.py:143
  26.7 2.2 select_reduce_fusion
  29.0 16.7 %collective-permute-done.1 = f32[16,128,128]{2,0,1:T(8,128)S(1)} collective-permute-done((f32[16,128,128]{2,0,1:T(8,128)S(1)}, f32[16,128,128]{2,0,1:T(8,128)S(1)}, u32[]{:S(2)}, u32[]{:S(2)}) %collective-permute-start.1) | collective-permute-done | bytes 1048608 | tf_op jit(solution)/shard_map/ppermute | solution.py:21
  45.6 21.9 %collective-permute-done = f32[16,128,128]{2,0,1:T(8,128)} collective-permute-done((f32[16,128,128]{2,0,1:T(8,128)S(1)}, f32[16,128,128]{2,0,1:T(8,128)}, u32[]{:S(2)}, u32[]{:S(2)}) %collective-permute-start) | collective-permute-done | bytes 1048608 | tf_op jit(solution)/shard_map/ppermute | solution.py:20
  67.5 3.4 fusion.4
  70.9 2.1 copy.50
  73.0 3.4 fusion.86
  78.1 9.8 %fusion.37 = f32[2,16,128,128]{3,2,1,0:T(8,128)} fusion(f32[1,16,128,128]{3,2,1,0:T(8,128)S(1)} %copy.46, f32[1,16,128,128]{3,2,1,0:T(8,128)} %param.7, f32[2,16,128,1,16]{2,4,1,0,3:T(8,128)S(1)} %broadcast.160, f32[2,16,128,1,128]{2,4,1,0,3:T(8,128)S(1)} %bitcast.130, f32[2,160,128]{2,1,0:T(8,128)} %get-tuple-element.6), kind=kOutput, calls=%fused_computation.54 | convolution fusion | flops 1008992256 | bytes 6717440 | tf_op jit(solution)/shard_map/vabns,vsi->vabni/dot_general | solution.py:53
  89.2 6.6 %collective-permute-start.2 = (f32[2,16,128,128]{3,2,1,0:T(8,128)}, f32[2,16,128,128]{3,2,1,0:T(8,128)}, u32[]{:S(2)}, u32[]{:S(2)}) collective-permute-start(f32[2,16,128,128]{3,2,1,0:T(8,128)} %fusion.37), channel_id=1, source_target_pairs={{0,4},{4,8},{8,12},{12,16},{16,20},{20,24},{24,28},{1,5},{5,9},{9,... | collective-permute-start | bytes 6291464 | tf_op jit(solution)/shard_map/ppermute | solution.py:20
  96.8 41.5 %collective-permute-done.3 = f32[2,16,128,128]{3,2,1,0:T(8,128)S(1)} collective-permute-done((f32[2,16,128,128]{3,2,1,0:T(8,128)}, f32[2,16,128,128]{3,2,1,0:T(8,128)S(1)}, u32[]{:S(2)}, u32[]{:S(2)}) %collective-permute-start.3) | collective-permute-done | bytes 2097184 | tf_op jit(solution)/shard_map/ppermute | solution.py:21
  138.3 45.2 %collective-permute-done.2 = f32[2,16,128,128]{3,2,1,0:T(8,128)} collective-permute-done((f32[2,16,128,128]{3,2,1,0:T(8,128)}, f32[2,16,128,128]{3,2,1,0:T(8,128)}, u32[]{:S(2)}, u32[]{:S(2)}) %collective-permute-start.2) | collective-permute-done | bytes 2097184 | tf_op jit(solution)/shard_map/ppermute | solution.py:20
  183.5 2.6 pad_maximum_fusion
  186.2 7.8 %fusion.2 = f32[2,16,128,128]{3,1,2,0:T(8,128)} fusion(f32[2,48,128,128]{3,2,1,0:T(8,128)S(1)} %pad_maximum_fusion, f32[2,48,16]{1,2,0:T(8,128)S(1)} %get-tuple-element.9), kind=kOutput, calls=%fused_computation.4 | convolution fusion | flops 301989888 | bytes 8394752 | tf_op jit(solution)/shard_map/vsyl,vsi->viyl/dot_general | solution.py:72
  194.0 2.4 copy.52
  198.3 7.4 %fusion.35 = f32[16,128,128]{2,1,0:T(8,128)S(1)} fusion(f32[2,16,128,1,16]{2,4,1,0,3:T(8,128)S(1)} %copy-done.5, f32[2,16,128,1,128]{2,4,1,0,3:T(8,128)S(1)} %bitcast.133, f32[2,128]{1,0:T(2,128)S(1)} %get-tuple-element.12, f32[2,16,128]{2,1,0:T(8,128)S(1)} %broadcast_multiply_fusion, f32[2,128]{1,0:T(2,128)S(1)} %pad_maximum_fusion.13, ...), kind=kOutput, calls=%fused_computation.52 | convolution fusion | flops 1009778688 | bytes 3590144 | tf_op jit(solution)/shard_map/vabns,vsi->vabni/dot_general | solution.py:53
  207.7 37.2 %all-reduce.3.cloned.1.call-done = f32[16,128,128]{2,0,1:T(8,128)} async-done(((f32[16,128,128]{2,0,1:T(8,128)}), f32[16,128,128]{2,0,1:T(8,128)}) %all-reduce.3.cloned.1.call-update) | async-done | bytes 1048592 | tf_op jit(solution)/shard_map/psum | solution.py:160
  244.9 1.9 exponential_multiply_fusion.1
  248.0 4.6 collective-permute-start.4
  252.7 20.7 %collective-permute-done.5 = f32[16,128,128]{2,0,1:T(8,128)S(1)} collective-permute-done((f32[16,128,128]{2,0,1:T(8,128)S(1)}, f32[16,128,128]{2,0,1:T(8,128)S(1)}, u32[]{:S(2)}, u32[]{:S(2)}) %collective-permute-start.5) | collective-permute-done | bytes 1048608 | tf_op jit(solution)/shard_map/ppermute | solution.py:21
  273.3 22.1 %collective-permute-done.4 = f32[16,128,128]{2,0,1:T(8,128)S(1)} collective-permute-done((f32[16,128,128]{2,0,1:T(8,128)S(1)}, f32[16,128,128]{2,0,1:T(8,128)S(1)}, u32[]{:S(2)}, u32[]{:S(2)}) %collective-permute-start.4) | collective-permute-done | bytes 1048608 | tf_op jit(solution)/shard_map/ppermute | solution.py:20
  295.4 1.9 fusion.9
  297.3 2.1 copy.57
  299.4 3.5 fusion.88
  303.0 7.0 %fusion.36 = f32[2,16,128,128]{3,2,1,0:T(8,128)S(1)} fusion(f32[1,16,128,128]{3,2,1,0:T(8,128)S(1)} %copy-done.3, f32[1,16,128,128]{3,2,1,0:T(8,128)S(1)} %copy-done.14, f32[2,16,128,1,16]{2,4,1,0,3:T(8,128)S(1)} %copy-done.6, f32[2,16,128,1,128]{2,4,1,0,3:T(8,128)S(1)} %bitcast.132, f32[2,160,128]{2,1,0:T(8,128)S(1)} %copy-done.10), kind=kOutput, calls=%fused_computation.53 | convolution fusion | flops 1008992256 | bytes 6717440 | tf_op jit(solution)/shard_map/vabns,vsi->vabni/dot_general | solution.py:53
  311.3 5.4 %collective-permute-start.6 = (f32[2,16,128,128]{3,2,1,0:T(8,128)S(1)}, f32[2,16,128,128]{3,2,1,0:T(8,128)S(1)}, u32[]{:S(2)}, u32[]{:S(2)}) collective-permute-start(f32[2,16,128,128]{3,2,1,0:T(8,128)S(1)} %fusion.36), channel_id=1, source_target_pairs={{0,4},{4,8},{8,12},{12,16},{16,20},{20,24},{24,28},{1,5},{5,9},{9,... | collective-permute-start | bytes 6291464 | tf_op jit(solution)/shard_map/ppermute | solution.py:20
  316.7 43.5 %collective-permute-done.7 = f32[2,16,128,128]{3,2,1,0:T(8,128)S(1)} collective-permute-done((f32[2,16,128,128]{3,2,1,0:T(8,128)S(1)}, f32[2,16,128,128]{3,2,1,0:T(8,128)S(1)}, u32[]{:S(2)}, u32[]{:S(2)}) %collective-permute-start.7) | collective-permute-done | bytes 2097184 | tf_op jit(solution)/shard_map/ppermute | solution.py:21
  360.2 45.1 %collective-permute-done.6 = f32[2,16,128,128]{3,2,1,0:T(8,128)S(1)} collective-permute-done((f32[2,16,128,128]{3,2,1,0:T(8,128)S(1)}, f32[2,16,128,128]{3,2,1,0:T(8,128)S(1)}, u32[]{:S(2)}, u32[]{:S(2)}) %collective-permute-start.6) | collective-permute-done | bytes 2097184 | tf_op jit(solution)/shard_map/ppermute | solution.py:20
  406.1 7.8 %fusion = f32[2,16,128,128]{3,1,2,0:T(8,128)} fusion(f32[2,48,128,128]{3,2,1,0:T(8,128)S(1)} %pad_maximum_fusion.1, f32[2,48,16]{1,2,0:T(8,128)S(1)} %get-tuple-element.9), kind=kOutput, calls=%fused_computation.2 | convolution fusion | flops 301989888 | bytes 8394752 | tf_op jit(solution)/shard_map/vsyl,vsi->viyl/dot_general | solution.py:72
  414.0 2.2 copy.59
  418.1 7.5 %fusion.34 = f32[16,128,128]{2,1,0:T(8,128)S(1)} fusion(f32[2,16,128,1,16]{2,4,1,0,3:T(8,128)S(1)} %copy-done.7, f32[2,16,128,1,128]{2,4,1,0,3:T(8,128)S(1)} %bitcast.131, f32[2,128]{1,0:T(2,128)S(1)} %get-tuple-element.12, f32[2,16,128]{2,1,0:T(8,128)S(1)} %broadcast_multiply_fusion, f32[2,128]{1,0:T(2,128)S(1)} %pad_maximum_fusion.13, ...), kind=kOutput, calls=%fused_computation.51 | convolution fusion | flops 1009778688 | bytes 3590144 | tf_op jit(solution)/shard_map/vabns,vsi->vabni/dot_general | solution.py:53
  427.1 37.1 %all-reduce.5.cloned.1.call-done = f32[16,128,128]{2,0,1:T(8,128)} async-done(((f32[16,128,128]{2,0,1:T(8,128)}), f32[16,128,128]{2,0,1:T(8,128)}) %all-reduce.5.cloned.1.call-update) | async-done | bytes 1048592 | tf_op jit(solution)/shard_map/psum | solution.py:160
  (82 shorter events, 25.5 us)
Async XLA Ops:
  8.4 37.3 %collective-permute-start.1 = (f32[16,128,128]{2,0,1:T(8,128)S(1)}, f32[16,128,128]{2,0,1:T(8,128)S(1)}, u32[]{:S(2)}, u32[]{:S(2)}) collective-permute-start(f32[16,128,128]{2,0,1:T(8,128)S(1)} %copy.56), channel_id=1, source_target_pairs={{4,0},{8,4},{12,8},{16,12},{20,16},{24,20},{28,24},{5,1},{9,5},{13... | collective-permute-start | bytes 3145736 | tf_op jit(solution)/shard_map/ppermute | solution.py:21
  9.7 57.8 %collective-permute-start = (f32[16,128,128]{2,0,1:T(8,128)S(1)}, f32[16,128,128]{2,0,1:T(8,128)}, u32[]{:S(2)}, u32[]{:S(2)}) collective-permute-start(f32[16,128,128]{2,0,1:T(8,128)S(1)} %copy.56), channel_id=1, source_target_pairs={{0,4},{4,8},{8,12},{12,16},{16,20},{20,24},{24,28},{1,5},{5,9},{9,... | collective-permute-start | bytes 3145736 | tf_op jit(solution)/shard_map/ppermute | solution.py:20
  17.7 6.4 %copy-start.12 = (f32[1,3,33]{2,0,1:T(1,128)S(1)}, f32[1,3,33]{2,0,1:T(1,128)}, u32[]{:S(2)}) copy-start(f32[1,3,33]{2,0,1:T(1,128)} %param.10) | copy-start | bytes 1192
  17.7 6.5 %copy-start.13 = (f32[1,3,33]{2,0,1:T(1,128)S(1)}, f32[1,3,33]{2,0,1:T(1,128)}, u32[]{:S(2)}) copy-start(f32[1,3,33]{2,0,1:T(1,128)} %param.9) | copy-start | bytes 1192
  18.8 57.6 %all-to-all-start = ((f32[1,16,128,8,16]{2,1,4,0,3:T(8,128)}), f32[1,16,128,8,16]{2,1,4,0,3:T(8,128)}, u32[]{:S(2)}, u32[]{:S(2)}) async-start(f32[1,16,128,8,16]{2,1,4,0,3:T(8,128)} %copy.44), calls=%async_computation | async-start | bytes 2097152 | tf_op jit(solution)/shard_map/all_to_all | solution.py:143
  24.0 220.8 %all-reduce.3.cloned.1.call-start = ((), (), s32[]{:S(2)}) async-start(), calls=%async_computation.1 | async-start | bytes 2097152 | tf_op jit(solution)/shard_map/psum | solution.py:160
  45.6 21.9 %copy-start.1 = (f32[16,128,128]{2,0,1:T(8,128)}, f32[16,128,128]{2,0,1:T(8,128)S(1)}, u32[]{:S(2)}) copy-start(f32[16,128,128]{2,0,1:T(8,128)S(1)} %collective-permute-done.1) | copy-start | bytes 3145732
  78.0 9.9 %copy-start.2 = (f32[1,16,128,128]{3,2,1,0:T(8,128)}, f32[1,16,128,128]{3,2,1,0:T(8,128)S(1)}, u32[]{:S(2)}) copy-start(f32[1,16,128,128]{3,2,1,0:T(8,128)S(1)} %copy.46) | copy-start | bytes 3145732
  78.1 9.8 %copy-start.4 = (f32[2,16,128,1,16]{2,4,1,0,3:T(8,128)}, f32[2,16,128,1,16]{2,4,1,0,3:T(8,128)S(1)}, u32[]{:S(2)}) copy-start(f32[2,16,128,1,16]{2,4,1,0,3:T(8,128)S(1)} %broadcast.160) | copy-start | bytes 786436
  78.1 17.9 %copy-start.11 = (s32[1,4,8]{2,1,0:T(4,128)S(1)}, s32[1,4,8]{2,1,0:T(4,128)}, u32[]{:S(2)}) copy-start(s32[1,4,8]{2,1,0:T(4,128)} %param.11) | copy-start | bytes 388
  87.9 50.4 %collective-permute-start.3 = (f32[2,16,128,128]{3,2,1,0:T(8,128)}, f32[2,16,128,128]{3,2,1,0:T(8,128)S(1)}, u32[]{:S(2)}, u32[]{:S(2)}) collective-permute-start(f32[2,16,128,128]{3,2,1,0:T(8,128)} %fusion.37), channel_id=1, source_target_pairs={{4,0},{8,4},{12,8},{16,12},{20,16},{24,20},{28,24},{5,1},{9,5},{13... | collective-permute-start | bytes 6291464 | tf_op jit(solution)/shard_map/ppermute | solution.py:21
  89.2 94.3 %collective-permute-start.2 = (f32[2,16,128,128]{3,2,1,0:T(8,128)}, f32[2,16,128,128]{3,2,1,0:T(8,128)}, u32[]{:S(2)}, u32[]{:S(2)}) collective-permute-start(f32[2,16,128,128]{3,2,1,0:T(8,128)} %fusion.37), channel_id=1, source_target_pairs={{0,4},{4,8},{8,12},{12,16},{16,20},{20,24},{24,28},{1,5},{5,9},{9,... | collective-permute-start | bytes 6291464 | tf_op jit(solution)/shard_map/ppermute | solution.py:20
  196.4 1.9 copy-start.5
  196.4 1.9 copy-start.8
  205.7 39.2 %copy-start = (f32[16,128,128]{2,1,0:T(8,128)S(1)}, f32[16,128,128]{2,1,0:T(8,128)}, u32[]{:S(2)}) copy-start(f32[16,128,128]{2,1,0:T(8,128)} %param.6) | copy-start | bytes 3145732
  207.3 256.9 %all-reduce.5.cloned.1.call-start = ((), (), s32[]{:S(2)}) async-start(), calls=%async_computation.2 | async-start | bytes 2097152 | tf_op jit(solution)/shard_map/psum | solution.py:160
  246.7 26.6 %collective-permute-start.5 = (f32[16,128,128]{2,0,1:T(8,128)S(1)}, f32[16,128,128]{2,0,1:T(8,128)S(1)}, u32[]{:S(2)}, u32[]{:S(2)}) collective-permute-start(f32[16,128,128]{2,0,1:T(8,128)S(1)} %exponential_multiply_fusion.1), channel_id=1, source_target_pairs={{4,0},{8,4},{12,8},{16,12},{20,16},{24,20},{28,24},{5,1},{9,5},{13... | collective-permute-start | bytes 3145736 | tf_op jit(solution)/shard_map/ppermute | solution.py:21
  248.0 47.4 %collective-permute-start.4 = (f32[16,128,128]{2,0,1:T(8,128)S(1)}, f32[16,128,128]{2,0,1:T(8,128)S(1)}, u32[]{:S(2)}, u32[]{:S(2)}) collective-permute-start(f32[16,128,128]{2,0,1:T(8,128)S(1)} %exponential_multiply_fusion.1), channel_id=1, source_target_pairs={{0,4},{4,8},{8,12},{12,16},{16,20},{20,24},{24,28},{1,5},{5,9},{9,... | collective-permute-start | bytes 3145736 | tf_op jit(solution)/shard_map/ppermute | solution.py:20
  299.4 3.6 copy-start.3
  299.4 3.6 copy-start.6
  299.4 3.6 copy-start.10
  299.4 3.6 copy-start.14
  310.0 50.2 %collective-permute-start.7 = (f32[2,16,128,128]{3,2,1,0:T(8,128)S(1)}, f32[2,16,128,128]{3,2,1,0:T(8,128)S(1)}, u32[]{:S(2)}, u32[]{:S(2)}) collective-permute-start(f32[2,16,128,128]{3,2,1,0:T(8,128)S(1)} %fusion.36), channel_id=1, source_target_pairs={{4,0},{8,4},{12,8},{16,12},{20,16},{24,20},{28,24},{5,1},{9,5},{13... | collective-permute-start | bytes 6291464 | tf_op jit(solution)/shard_map/ppermute | solution.py:21
  311.3 94.0 %collective-permute-start.6 = (f32[2,16,128,128]{3,2,1,0:T(8,128)S(1)}, f32[2,16,128,128]{3,2,1,0:T(8,128)S(1)}, u32[]{:S(2)}, u32[]{:S(2)}) collective-permute-start(f32[2,16,128,128]{3,2,1,0:T(8,128)S(1)} %fusion.36), channel_id=1, source_target_pairs={{0,4},{4,8},{8,12},{12,16},{16,20},{20,24},{24,28},{1,5},{5,9},{9,... | collective-permute-start | bytes 6291464 | tf_op jit(solution)/shard_map/ppermute | solution.py:20
  416.2 1.9 copy-start.7
  416.2 1.9 copy-start.9
Sparse Core Ops, SparseCore 0:
  207.4 37.3 all-reduce.2
  427.3 36.8 all-reduce.4
where the time goes:
time: 480 us; the launch traced here: 474 us
  waiting for transfers between devices  331 us (69%)
  matrix products  63.6 us (13%)
  starting transfers between devices  33.5 us (7%)
  local copies, waits for them, and re-layouts  19.9 us (4%)
  between operations  14.2 us (3%)
  other arithmetic  11.8 us (2%)
    ppermute x4, waiting for transfers between devices, extended(): before = lax.ppermute(last, axis, up)  134 us
    ppermute x4, waiting for transfers between devices, extended(): after = lax.ppermute(leading, axis, down)  122 us
    psum x2, waiting for transfers between devices, local(): log_total = lax.psum(log_total, 'view')  74.3 us
    dot_general x4, matrix products, along_last(): jnp.einsum('vabns,vsi->vabni', windows, band_matrix(kernel, block_width),...  31.7 us
    ppermute x4, starting transfers between devices, extended(): before = lax.ppermute(last, axis, up)  23 us
    dot_general x2, matrix products, backward(): jnp.einsum('vsyl,vsi->viyl', padded, band_matrix(kernel_first, plane_coun...  15.7 us
    unnamed x4, matrix products  10.6 us
  transfers between devices with their start and end apart: 11, of which 10 were waited for; matrix products, arithmetic and copies ran while one was open for 4% of the time, Pallas kernels for 0%

commit v1 on v0

--- a/solution.py
+++ b/solution.py
@@ -1,6 +1,10 @@
+import functools
+
 import jax
 import jax.numpy as jnp
 from jax import lax
+from jax.experimental import pallas as pl
+from jax.experimental.pallas import tpu as pltpu
 from jax.sharding import PartitionSpec as P
 
 VA = 4
@@ -162,6 +166,571 @@
     return estimate
 
 
+F32 = jnp.float32
+BF16 = jnp.bfloat16
+MESH = pl.DeviceIdType.MESH
+
+
+def split_bf16(values):
+    high = values.astype(BF16)
+    low = (values - high.astype(F32)).astype(BF16)
+    return high, low
+
+
+def dot32(left, right):
+    return jnp.dot(left, right, preferred_element_type=F32)
+
+
+def joint_kernel(
+    owners,
+    views,
+    planes,
+    lines,
+    columns,
+    psf_ref,
+    estimate_ref,
+    axial_ref,
+    lateral_ref,
+    cover_ref,
+    out_ref,
+    window,
+    observed,
+    turned,
+    mid,
+    quot,
+    logs,
+    pair_sum,
+    peer_sum,
+    cover,
+    x_fwd,
+    x_back,
+    y_fwd,
+    y_back,
+    z_fwd,
+    z_back,
+    log_xy,
+    log_z,
+    weight,
+    cover_sem,
+    axial_sem,
+    lateral_sem,
+    edge_sem,
+    share_sem,
+    pair_sem,
+    peer_sem,
+):
+    taps = psf_ref.shape[0] // 3
+    rim = (taps - 1) // 2
+    groups = owners // 2
+    span = 2 * planes
+    block = planes // views
+    slab = columns // owners
+
+    me = lax.axis_index("owner")
+    view = lax.axis_index("view")
+    group = me // 2
+    side = lax.rem(me, 2)
+    core = lax.rem(view, 2)
+    row = view // 2
+    takes_lateral = lax.rem(side + core, 2)
+    has_below = group > 0
+    has_above = group < groups - 1
+
+    def device(side_, view_):
+        return (2 * group + side_, view_)
+
+    sibling = device(side, 2 * row + 1 - core)
+
+    barrier = pltpu.get_barrier_semaphore()
+    for step in range(1, owners):
+        pl.semaphore_signal(
+            barrier, inc=1, device_id=(lax.rem(me + step, owners), view), device_id_type=MESH
+        )
+    for side_ in (side, 1 - side):
+        for step in range(1, views):
+            pl.semaphore_signal(
+                barrier,
+                inc=1,
+                device_id=device(side_, lax.rem(view + step, views)),
+                device_id_type=MESH,
+            )
+    own_rows = pl.ds((planes + planes * side) * lines, planes * lines)
+    window[own_rows, :] = estimate_ref[...]
+    cover[pl.ds(side, 1)] = cover_ref[...][None]
+    pl.semaphore_wait(barrier, owners - 1 + 2 * (views - 1))
+
+    def remote(src, dst, sems, index, target):
+        return pltpu.make_async_remote_copy(
+            src_ref=src,
+            dst_ref=dst,
+            send_sem=sems.at[0, index],
+            recv_sem=sems.at[1, index],
+            device_id=target,
+            device_id_type=MESH,
+        )
+
+    def window_rows(e):
+        return pl.ds(e * (block * lines), block * lines)
+
+    def share(stage, first, last):
+        def copy(e_src, e_dst, slot, target):
+            return pltpu.make_async_remote_copy(
+                src_ref=window.at[window_rows(e_src)],
+                dst_ref=window.at[window_rows(e_dst)],
+                send_sem=share_sem.at[0, stage, slot],
+                recv_sem=share_sem.at[1, stage, e_dst],
+                device_id=target,
+                device_id_type=MESH,
+            )
+
+        def arrival(e):
+            return copy(e, e, 0, sibling)
+
+        def slot_of(side_, row_, core_):
+            return views + views * side_ + 2 * row_ + core_
+
+        own = slot_of(side, row, core)
+        sent = []
+
+        def start(condition, made):
+            if condition is None:
+                made.start()
+            else:
+                pl.when(condition)(made.start)
+            sent.append((condition, made))
+
+        if not first:
+            start(None, copy(own, own, 0, device(side, 2 * (1 - row) + core)))
+        if not last:
+            start(None, copy(own, own, 1, device(1 - side, view)))
+            start(None, copy(own, own, 2, device(1 - side, 2 * (1 - row) + core)))
+        if not first:
+            start(None, copy(own, own, 3, sibling))
+        slot = 4
+        kinds = [(0, 0), (0, 1)] if last else [(0, 0), (1, 0), (0, 1), (1, 1)]
+        if first:
+            kinds = [(0, 0), (0, 1), (1, 0), (1, 1)]
+        for d_side, d_row in kinds:
+            side_ = lax.rem(side + d_side, 2)
+            row_ = lax.rem(row + d_row, 2)
+            e = slot_of(side_, row_, core)
+            is_own = (d_side, d_row) == (0, 0)
+            if not is_own and not (first and d_side == 0):
+                arrival(e).wait_recv()
+            if not last:
+                to = group + 2 * side_ - 1
+                valid = (to >= 0) & (to < groups)
+                e_dst = (1 - side_) * 3 * views + 2 * row_ + core
+                start(valid, copy(e, e_dst, slot, (2 * to + side, view)))
+                slot += 1
+            if not is_own and not (first and d_side == 0):
+                start(None, copy(e, e, slot, sibling))
+                slot += 1
+        if not last:
+            for row_ in (0, 1):
+                for base, condition in ((0, has_below), (3 * views, has_above)):
+                    e = base + 2 * row_ + core
+                    made = copy(e, e, slot, sibling)
+                    pl.when(condition)(arrival(e).wait_recv)
+                    start(condition, made)
+                    slot += 1
+        other = 1 - core
+        for d_side, d_row in kinds:
+            if first and d_side == 0:
+                continue
+            side_ = lax.rem(side + d_side, 2)
+            row_ = lax.rem(row + d_row, 2)
+            arrival(slot_of(side_, row_, other)).wait_recv()
+        if not last:
+            for row_ in (0, 1):
+                pl.when(has_below)(arrival(2 * row_ + other).wait_recv)
+                pl.when(has_above)(arrival(3 * views + 2 * row_ + other).wait_recv)
+        for condition, made in sent:
+            if condition is None:
+                made.wait_send()
+            else:
+                pl.when(condition)(made.wait_send)
+
+    def toeplitz(axis, shape, offset, flip):
+        first = lax.broadcasted_iota(jnp.int32, shape, 0)
+        second = lax.broadcasted_iota(jnp.int32, shape, 1)
+        place = (second - first if flip else first - second) + (rim + offset)
+
+        def add(t, total):
+            return jnp.where(place == t, psf_ref[axis * taps + t], total)
+
+        return lax.fori_loop(0, taps, add, jnp.zeros(shape, F32))
+
+    def store_right(ref, matrix):
+        high, low = split_bf16(matrix)
+        top = jnp.concatenate([high, low], axis=1)
+        ref[...] = jnp.concatenate([top, top], axis=0)
+
+    def store_left(ref, matrix):
+        high, low = split_bf16(matrix)
+        ref[...] = jnp.concatenate(
+            [jnp.concatenate([high, high], axis=1), jnp.concatenate([low, low], axis=1)], axis=0
+        )
+
+    def prepare():
+        store_right(x_fwd, toeplitz(2, (columns, columns), 0, False))
+        back_x = toeplitz(2, (columns, columns), 0, True)
+        store_right(x_back, back_x)
+        store_left(y_fwd, toeplitz(1, (lines, lines), 0, True))
+        back_y = toeplitz(1, (lines, lines), 0, False)
+        store_left(y_back, back_y)
+        store_left(z_fwd, toeplitz(0, (span, 2 * span), -planes, True))
+        back_z = toeplitz(0, (span, 2 * span), planes, False)
+        store_left(z_back, back_z)
+        log_xy[...] = jnp.log(jnp.sum(back_y, axis=1, keepdims=True)) + jnp.log(
+            jnp.sum(back_x, axis=0, keepdims=True)
+        )
+        plane = lax.broadcasted_iota(jnp.int32, (span, 2 * span), 1) + (group * span - planes)
+        inside = (plane >= 0) & (plane < owners * planes)
+        sums = jnp.sum(jnp.where(inside, back_z, 0.0), axis=1, keepdims=True)
+        log_z[...] = jnp.broadcast_to(jnp.log(sums), (span, columns))
+
+    cover_copy = remote(cover.at[side], cover.at[side], cover_sem, 0, device(1 - side, view))
+    cover_copy.start()
+    axial_target = device(core, view)
+    axial_mine = pl.ds(side * planes, planes)
+    axial_copy = remote(axial_ref, observed.at[axial_mine], axial_sem, 0, axial_target)
+
+    def lateral_copy(to):
+        return pltpu.make_async_remote_copy(
+            src_ref=turned.at[pl.ds(to * span, span)],
+            dst_ref=observed.at[:, pl.ds(me * slab, slab), :],
+            send_sem=lateral_sem.at[0, to],
+            recv_sem=lateral_sem.at[1, me],
+            device_id=(2 * to + 1 - core, view),
+            device_id_type=MESH,
+        )
+
+    def lateral_arrival(source):
+        return pltpu.make_async_remote_copy(
+            src_ref=observed.at[:, pl.ds(source * slab, slab), :],
+            dst_ref=observed.at[:, pl.ds(source * slab, slab), :],
+            send_sem=lateral_sem.at[0, 0],
+            recv_sem=lateral_sem.at[1, source],
+            device_id=sibling,
+            device_id_type=MESH,
+        )
+
+    def turn():
+        for x in range(slab):
+            turned[:, x, :] = lateral_ref[x].T
+
+    def start_views():
+        @pl.when(takes_lateral == 1)
+        def _():
+            axial_copy.start()
+
+        for to in range(groups):
+
+            @pl.when((takes_lateral == 0) | (to != group))
+            def _():
+                lateral_copy(to).start()
+
+    def finish_views():
+        @pl.when(takes_lateral == 1)
+        def _():
+            observed[:, pl.ds(pl.multiple_of(me * slab, slab), slab), :] = turned[
+                pl.ds(group * span, span)
+            ]
+            axial_copy.wait_send()
+            for step in range(1, owners):
+                lateral_arrival(lax.rem(me + step, owners)).wait_recv()
+
+            def flip(z, carry):
+                observed[z] = observed[z].T
+                return carry
+
+            lax.fori_loop(0, span, flip, 0)
+
+        @pl.when(takes_lateral == 0)
+        def _():
+            observed[axial_mine] = axial_ref[...]
+            theirs = observed.at[pl.ds((1 - side) * planes, planes)]
+            remote(theirs, theirs, axial_sem, 0, sibling).wait_recv()
+
+        for to in range(groups):
+
+            @pl.when((takes_lateral == 0) | (to != group))
+            def _():
+                lateral_copy(to).wait_send()
+
+    def along_z(source, matrix, y):
+        both = jnp.concatenate(
+            [
+                source[pl.ds(y, 2 * span, stride=lines), :],
+                source[pl.ds(y + 1, 2 * span, stride=lines), :],
+            ],
+            axis=1,
+        )
+        high, low = split_bf16(both)
+        result = dot32(matrix[...], jnp.concatenate([high, low], axis=0))
+        result = result[:span] + result[span:]
+        return result[:, :columns], result[:, columns:]
+
+    def along_x(planes_two, matrix):
+        high, low = split_bf16(planes_two)
+        result = dot32(jnp.concatenate([high, low], axis=1), matrix[...])
+        return result[:, :columns] + result[:, columns:]
+
+    def along_y(planes_two, matrix):
+        high, low = split_bf16(planes_two)
+        result = dot32(matrix[...], jnp.concatenate([high, low], axis=0))
+        return result[:lines] + result[lines:]
+
+    def side_by_side(stacked):
+        return jnp.concatenate([stacked[:lines], stacked[lines:]], axis=1)
+
+    def stacked_up(beside):
+        return jnp.concatenate([beside[:, :columns], beside[:, columns:]], axis=0)
+
+    def forward_z():
+        def lines_of(i, carry):
+            for part in range(4):
+                y = i * 8 + 2 * part
+                one, two = along_z(window, z_fwd, y)
+                mid[pl.ds(y, span, stride=lines), :] = one
+                mid[pl.ds(y + 1, span, stride=lines), :] = two
+            return carry
+
+        lax.fori_loop(0, lines // 8, lines_of, 0)
+
+    def plane_pair(iteration, z):
+        rows = pl.ds(pl.multiple_of(z * lines, 2 * lines), 2 * lines)
+        blurred = along_x(mid[rows, :], x_fwd)
+        blurred = along_y(side_by_side(blurred), y_fwd)
+        seen = jnp.concatenate([observed[z], observed[z + 1]], axis=1)
+        back = along_y(seen / blurred, y_back)
+        back = along_x(stacked_up(back), x_back)
+        there = pl.ds(pl.multiple_of((planes + z) * lines, 2 * lines), 2 * lines)
+        quot[iteration, there, :] = back
+
+    def edge(iteration, s, up):
+        start = (2 * planes if up else planes) + 2 * s
+        end = (0 if up else 3 * planes) + 2 * s
+        to = me + 2 if up else me - 2
+        way = 1 if up else 0
+        return pltpu.make_async_remote_copy(
+            src_ref=quot.at[iteration, pl.ds(start * lines, 2 * lines)],
+            dst_ref=quot.at[iteration, pl.ds(end * lines, 2 * lines)],
+            send_sem=edge_sem.at[0, iteration, way, s],
+            recv_sem=edge_sem.at[1, iteration, way, s],
+            device_id=(to, view),
+            device_id_type=MESH,
+        )
+
+    def middle(iteration):
+        def step(s, carry):
+            plane_pair(iteration, 2 * s)
+            plane_pair(iteration, planes + 2 * s)
+            pl.when(has_below)(edge(iteration, s, False).start)
+            pl.when(has_above)(edge(iteration, s, True).start)
+            return carry
+
+        lax.fori_loop(0, planes // 2, step, 0)
+
+        def finish(s, carry):
+            @pl.when(has_below)
+            def _():
+                edge(iteration, s, False).wait_send()
+                edge(iteration, s, True).wait_recv()
+
+            @pl.when(has_above)
+            def _():
+                edge(iteration, s, True).wait_send()
+                edge(iteration, s, False).wait_recv()
+
+            return carry
+
+        lax.fori_loop(0, planes // 2, finish, 0)
+
+    def backward_z(iteration):
+        source = quot.at[iteration]
+
+        def lines_of(i, carry):
+            for part in range(4):
+                y = i * 8 + 2 * part
+                for step, back in enumerate(along_z(source, z_back, y)):
+                    value = jnp.log(back) - (log_z[...] + log_xy[pl.ds(y + step, 1), :])
+                    logs[pl.ds(y + step, span, stride=lines), :] = weight[...] * value
+            return carry
+
+        lax.fori_loop(0, lines // 8, lines_of, 0)
+
+    def block_rows(b):
+        return pl.ds(pl.multiple_of(b * (block * lines), block * lines), block * lines)
+
+    def reduce_and_update(iteration):
+        kinds = [(1, 1), (1, 0), (0, 1), (0, 0)]
+
+        def log_block(kind, core_):
+            side_ = lax.rem(side + kind[0], 2)
+            row_ = lax.rem(row + kind[1], 2)
+            return views * side_ + 2 * row_ + core_
+
+        def to_sibling(k):
+            return pltpu.make_async_remote_copy(
+                src_ref=logs.at[block_rows(log_block(kinds[k], 1 - core))],
+                dst_ref=pair_sum.at[iteration, k],
+                send_sem=pair_sem.at[0, iteration, k],
+                recv_sem=pair_sem.at[1, iteration, k],
+                device_id=sibling,
+                device_id_type=MESH,
+            )
+
+        def to_peer(k):
+            side_ = lax.rem(side + kinds[k][0], 2)
+            row_ = lax.rem(row + kinds[k][1], 2)
+            return pltpu.make_async_remote_copy(
+                src_ref=logs.at[block_rows(log_block(kinds[k], core))],
+                dst_ref=peer_sum.at[iteration, k],
+                send_sem=peer_sem.at[0, iteration, k],
+                recv_sem=peer_sem.at[1, iteration, k],
+                device_id=device(side_, 2 * row_ + core),
+                device_id_type=MESH,
+            )
+
+        for k in range(4):
+            to_sibling(k).start()
+        for k in range(4):
+            to_sibling(k).wait_recv()
+            mine = block_rows(log_block(kinds[k], core))
+            logs[mine, :] = logs[mine, :] + pair_sum[iteration, k]
+            if k < 3:
+                to_peer(k).start()
+        for k in (1, 2, 0):
+            to_peer(k).wait_recv()
+        count = jnp.sum(cover_ref[...], axis=0, keepdims=True)
+        mine = block_rows(views * side + view)
+        total = logs[mine, :] + peer_sum[iteration, 0] + peer_sum[iteration, 1] + peer_sum[iteration, 2]
+        here = window_rows(views + views * side + view)
+        window[here, :] = window[here, :] * jnp.exp(total / count)
+        for k in range(4):
+            to_sibling(k).wait_send()
+        for k in range(3):
+            to_peer(k).wait_send()
+
+    turn()
+    start_views()
+
+    @pl.when(group == 0)
+    def _():
+        below = pl.ds(0, planes * lines)
+        window[below, :] = jnp.zeros((planes * lines, columns), F32)
+        for iteration in range(ITERS):
+            quot[iteration, below, :] = jnp.zeros((planes * lines, columns), F32)
+
+    @pl.when(group == groups - 1)
+    def _():
+        above = pl.ds(3 * planes * lines, planes * lines)
+        window[above, :] = jnp.zeros((planes * lines, columns), F32)
+        for iteration in range(ITERS):
+            quot[iteration, above, :] = jnp.zeros((planes * lines, columns), F32)
+
+    share(0, True, False)
+    prepare()
+    forward_z()
+    cover_copy.wait_send()
+    remote(cover.at[1 - side], cover.at[1 - side], cover_sem, 0, sibling).wait_recv()
+    which = takes_lateral * views + view
+    weight[:planes, :] = jnp.broadcast_to(cover[0, pl.ds(which, 1), :], (planes, columns))
+    weight[planes:, :] = jnp.broadcast_to(cover[1, pl.ds(which, 1), :], (planes, columns))
+    finish_views()
+    for iteration in range(ITERS):
+        if iteration > 0:
+            forward_z()
+        middle(iteration)
+        backward_z(iteration)
+        reduce_and_update(iteration)
+        share(iteration + 1, False, iteration == ITERS - 1)
+    out_ref[...] = window[own_rows, :]
+
+
+def joint(estimate, axial_views, lateral_views, psf_axial, psf_lateral, coverage):
+    planes, lines, columns = estimate.shape
+    owners = lax.axis_size("owner")
+    views = lax.axis_size("view")
+    slab = columns // owners
+    span = 2 * planes
+    depth = owners * planes
+    block_rows = planes // views * lines
+    takes_lateral = (lax.axis_index("owner") + lax.axis_index("view")) % 2 == 1
+    psf = jnp.where(takes_lateral, psf_lateral[0], psf_axial[0])
+    psf = psf / jnp.sum(psf, axis=-1, keepdims=True)
+    cover = jnp.repeat(coverage[0].astype(F32).T, columns // coverage.shape[1], axis=1)
+    vmem = pl.BlockSpec(memory_space=pltpu.VMEM)
+    dma = pltpu.SemaphoreType.DMA
+    result = pl.pallas_call(
+        functools.partial(joint_kernel, owners, views, planes, lines, columns),
+        out_shape=jax.ShapeDtypeStruct((planes * lines, columns), F32),
+        in_specs=[pl.BlockSpec(memory_space=pltpu.SMEM)] + [vmem] * 4,
+        out_specs=vmem,
+        scratch_shapes=[
+            pltpu.VMEM((2 * span * lines, columns), F32),
+            pltpu.VMEM((span, lines, columns), F32),
+            pltpu.VMEM((depth, slab, lines), F32),
+            pltpu.VMEM((span * lines, columns), F32),
+            pltpu.VMEM((ITERS, 2 * span * lines, columns), F32),
+            pltpu.VMEM((span * lines, columns), F32),
+            pltpu.VMEM((ITERS, 4, block_rows, columns), F32),
+            pltpu.VMEM((ITERS, 3, block_rows, columns), F32),
+            pltpu.VMEM((2,) + cover.shape, F32),
+            pltpu.VMEM((2 * columns, 2 * columns), BF16),
+            pltpu.VMEM((2 * columns, 2 * columns), BF16),
+            pltpu.VMEM((2 * lines, 2 * lines), BF16),
+            pltpu.VMEM((2 * lines, 2 * lines), BF16),
+            pltpu.VMEM((2 * span, 4 * span), BF16),
+            pltpu.VMEM((2 * span, 4 * span), BF16),
+            pltpu.VMEM((lines, columns), F32),
+            pltpu.VMEM((span, columns), F32),
+            pltpu.VMEM((span, columns), F32),
+            dma((2, 1)),
+            dma((2, 1)),
+            dma((2, owners)),
+            dma((2, ITERS, 2, planes // 2)),
+            dma((2, ITERS + 1, 4 * views)),
+            dma((2, ITERS, 4)),
+            dma((2, ITERS, 4)),
+        ],
+        compiler_params=pltpu.CompilerParams(
+            collective_id=0, has_side_effects=True, vmem_limit_bytes=48 * 1024 * 1024
+        ),
+    )(
+        psf.reshape(-1),
+        estimate.reshape(planes * lines, columns),
+        axial_views[0],
+        lateral_views[0],
+        cover,
+    )
+    return result.reshape(planes, lines, columns)
+
+
+def chosen(estimate, axial_views, lateral_views, psf_axial, psf_lateral, coverage):
+    planes, lines, columns = estimate.shape
+    owners = lax.axis_size("owner")
+    views = lax.axis_size("view")
+    rim = (psf_axial.shape[-1] - 1) // 2
+    fits = (
+        lines == columns
+        and columns % 128 == 0
+        and planes * lines * columns * 4 <= 1024 * 1024
+        and planes * owners == columns
+        and axial_views.shape[0] == 1
+        and lateral_views.shape[0] == 1
+        and views == 4
+        and owners % 2 == 0
+        and planes % views == 0
+        and rim <= planes
+        and columns // owners % 8 == 0
+    )
+    body = joint if fits else local
+    return body(estimate, axial_views, lateral_views, psf_axial, psf_lateral, coverage)
+
+
 def solution(mesh):
     in_specs = (
         P("owner", None, None),
@@ -172,4 +741,4 @@
         P("owner", None, None),
     )
     out_specs = P("owner", None, None)
-    return jax.shard_map(local, mesh=mesh, in_specs=in_specs, out_specs=out_specs, check_vma=False)
+    return jax.shard_map(chosen, mesh=mesh, in_specs=in_specs, out_specs=out_specs, check_vma=False)

time: 480 us -> 194 us (0.40); the launches traced: 474 us -> 194 us
  waiting for transfers between devices: 331 us -> 0 us
  Pallas kernels: 0 us -> 187 us
  matrix products: 63.6 us -> 0 us
  starting transfers between devices: 33.5 us -> 0 us
  between operations: 14.2 us -> 0.02 us
  local copies, waits for them, and re-layouts: 19.9 us -> 6.42 us
  other arithmetic: 11.8 us -> 0.12 us
    ppermute x8 -> x0, waiting for transfers between devices: 257 us -> none  [the longest x4 134 us: extended(): before = lax.ppermute(last, axis, up)]
    pallas_call x0 -> x1, Pallas kernels: none -> 187 us  [joint(): pl.pallas_call(functools.partial(joint_kernel, owners, views, planes, lin...]
    psum x2 -> x0, waiting for transfers between devices: 74.3 us -> none  [local(): log_total = lax.psum(log_total, 'view')]
    dot_general x10 -> x0, matrix products: 53 us -> none  [the longest x4 31.7 us: along_last(): jnp.einsum('vabns,vsi->vabni', windows, band_matrix(kernel, block_width),...]
    ppermute x8 -> x0, starting transfers between devices: 28.2 us -> none  [the longest x4 23 us: extended(): before = lax.ppermute(last, axis, up)]
    unnamed x4 -> x0, matrix products: 10.6 us -> none
    dot_general x4 -> x0, local copies, waits for them, and re-layouts: 8.8 us -> none  [the longest x2 4.58 us: backward(): jnp.einsum('vsyl,vsi->viyl', padded, band_matrix(kernel_first, plane_coun...]
    all_to_all x1 -> x0, starting transfers between devices: 5.23 us -> none  [local(): lax.all_to_all(moved_views, 'owner', split_axis=3, concat_axis=4, tiled=T...]
  transfers between devices with their start and end apart: 11 -> 0, of which waited for: 10 -> 0; matrix products, arithmetic and copies ran while one was open for 4% -> 0% of each run, Pallas kernels for 0% -> 0%
where the time goes in v1:
time: 194 us
  Pallas kernels  187 us (96%)
  local copies, waits for them, and re-layouts  6.42 us (3%)
    pallas_call x1, Pallas kernels, joint(): pl.pallas_call(functools.partial(joint_kernel, owners, views, planes, lin...  187 us
    unnamed x13, local copies, waits for them, and re-layouts  5.95 us

profile of v1, /device:TPU:0, one launch (start us, length us, event | category | flops | bytes accessed | tf_op | source)
XLA Modules:
  0.0 193.7 jit_solution(3896024577675674016)
XLA Ops:
  0.0 0.0 copy-start.3
  0.0 0.7 copy-done.3
  0.7 0.0 copy-start.4
  0.7 0.0 copy-start.5
  0.7 0.1 copy.7
  0.8 0.6 copy-done.4
  1.4 0.0 copy-done.5
  1.4 0.1 fusion
  1.5 0.1 select_n.23
  1.6 0.1 div.11
  1.6 0.1 div.12
  1.7 0.1 broadcast_in_dim.4
  1.8 0.1 reshape.20.cover_ref
  1.9 0.0 copy-start
  1.9 1.2 copy-done
  3.1 0.0 copy-start.1
  3.1 1.2 copy-done.1
  4.4 0.0 copy-start.2
  4.4 1.2 copy-done.2
  5.6 187.2 %shard_map.64 = f32[2048,128]{1,0:T(8,128)S(1)} custom-call(f32[99]{0:T(128)S(1)} %div.13.psf_ref, f32[2048,128]{1,0:T(8,128)S(1)} %bitcast.9, f32[16,128,128]{2,1,0:T(8,128)S(1)} %bitcast.10, f32[16,128,128]{2,1,0:T(8,128)S(1)} %bitcast.11, f32[8,128]{1,0:T(8,128)S(1)} %reshape.20.cover_ref), custom_call_target="tpu_custom_call" | custom-call | tf_op jit(solution)/shard_map/pallas_call | solution.py:667
  192.8 1.0 copy.9
  (2 shorter events, 0.0 us)
Async XLA Ops:
  0.0 0.7 copy-start.3
  0.7 0.7 copy-start.4
  0.7 0.7 copy-start.5
  1.9 1.2 copy-start
  3.1 1.2 copy-start.1
  4.4 1.2 copy-start.2

commit v2 on v1

--- a/solution.py
+++ b/solution.py
@@ -169,6 +169,7 @@
 F32 = jnp.float32
 BF16 = jnp.bfloat16
 MESH = pl.DeviceIdType.MESH
+CHUNKS = 4
 
 
 def split_bf16(values):
@@ -224,6 +225,7 @@
     groups = owners // 2
     span = 2 * planes
     block = planes // views
+    chunk_lines = lines // CHUNKS
     slab = columns // owners
 
     me = lax.axis_index("owner")
@@ -254,8 +256,8 @@
                 device_id=device(side_, lax.rem(view + step, views)),
                 device_id_type=MESH,
             )
-    own_rows = pl.ds((planes + planes * side) * lines, planes * lines)
-    window[own_rows, :] = estimate_ref[...]
+    own_planes = pl.ds(planes + planes * side, planes)
+    window[own_planes] = estimate_ref[...]
     cover[pl.ds(side, 1)] = cover_ref[...][None]
     pl.semaphore_wait(barrier, owners - 1 + 2 * (views - 1))
 
@@ -269,83 +271,106 @@
             device_id_type=MESH,
         )
 
-    def window_rows(e):
-        return pl.ds(e * (block * lines), block * lines)
-
-    def share(stage, first, last):
-        def copy(e_src, e_dst, slot, target):
-            return pltpu.make_async_remote_copy(
-                src_ref=window.at[window_rows(e_src)],
-                dst_ref=window.at[window_rows(e_dst)],
-                send_sem=share_sem.at[0, stage, slot],
-                recv_sem=share_sem.at[1, stage, e_dst],
-                device_id=target,
-                device_id_type=MESH,
-            )
-
-        def arrival(e):
-            return copy(e, e, 0, sibling)
-
-        def slot_of(side_, row_, core_):
-            return views + views * side_ + 2 * row_ + core_
-
-        own = slot_of(side, row, core)
-        sent = []
-
-        def start(condition, made):
-            if condition is None:
-                made.start()
-            else:
-                pl.when(condition)(made.start)
-            sent.append((condition, made))
-
+    def chunk(c):
+        return pl.ds(c * chunk_lines, chunk_lines)
+
+    def part(e, c):
+        return window.at[pl.ds(e * block, block), chunk(c)]
+
+    def slot_of(side_, row_, core_):
+        return views + views * side_ + 2 * row_ + core_
+
+    def copy_part(stage, c, e_src, e_dst, slot, target):
+        return pltpu.make_async_remote_copy(
+            src_ref=part(e_src, c),
+            dst_ref=part(e_dst, c),
+            send_sem=share_sem.at[0, stage, c, slot],
+            recv_sem=share_sem.at[1, stage, c, e_dst],
+            device_id=target,
+            device_id_type=MESH,
+        )
+
+    def arrival(stage, c, e):
+        return copy_part(stage, c, e, e, 0, sibling)
+
+    sent = {}
+
+    def start(stage, c, condition, *where):
+        made = copy_part(stage, c, *where)
+        if condition is None:
+            made.start()
+        else:
+            pl.when(condition)(made.start)
+        sent.setdefault((stage, c), []).append((condition, where))
+
+    own = slot_of(side, row, core)
+    row_peer = device(side, 2 * (1 - row) + core)
+    side_peer = device(1 - side, view)
+    far_peer = device(1 - side, 2 * (1 - row) + core)
+
+    def block_of(kind):
+        side_ = lax.rem(side + kind[0], 2)
+        row_ = lax.rem(row + kind[1], 2)
+        return side_, row_, slot_of(side_, row_, core)
+
+    def send_beside(stage, c, kind, slot):
+        side_, row_, e = block_of(kind)
+        to = group + 2 * side_ - 1
+        valid = (to >= 0) & (to < groups)
+        e_dst = (1 - side_) * 3 * views + 2 * row_ + core
+        start(stage, c, valid, e, e_dst, slot, (2 * to + side, view))
+
+    def spread_own(stage, c):
+        first, last = stage == 0, stage == ITERS
+        if not last:
+            start(stage, c, None, own, own, 0, side_peer)
         if not first:
-            start(None, copy(own, own, 0, device(side, 2 * (1 - row) + core)))
+            start(stage, c, None, own, own, 1, row_peer)
+            start(stage, c, None, own, own, 2, sibling)
+        if not first and not last:
+            start(stage, c, None, own, own, 3, far_peer)
         if not last:
-            start(None, copy(own, own, 1, device(1 - side, view)))
-            start(None, copy(own, own, 2, device(1 - side, 2 * (1 - row) + core)))
-        if not first:
-            start(None, copy(own, own, 3, sibling))
-        slot = 4
-        kinds = [(0, 0), (0, 1)] if last else [(0, 0), (1, 0), (0, 1), (1, 1)]
+            send_beside(stage, c, (0, 0), 4)
         if first:
-            kinds = [(0, 0), (0, 1), (1, 0), (1, 1)]
-        for d_side, d_row in kinds:
-            side_ = lax.rem(side + d_side, 2)
-            row_ = lax.rem(row + d_row, 2)
-            e = slot_of(side_, row_, core)
-            is_own = (d_side, d_row) == (0, 0)
-            if not is_own and not (first and d_side == 0):
-                arrival(e).wait_recv()
+            send_beside(stage, c, (0, 1), 5)
+
+    def spread_group(stage, c):
+        first, last = stage == 0, stage == ITERS
+        kinds = [(0, 1), (1, 0), (1, 1)]
+        if first:
+            kinds = kinds[1:]
+        if last:
+            kinds = kinds[:1]
+        for kind in kinds:
+            e = block_of(kind)[2]
+            arrival(stage, c, e).wait_recv()
+            if first and kind == (1, 0):
+                start(stage, c, None, e, e, 3, row_peer)
             if not last:
-                to = group + 2 * side_ - 1
-                valid = (to >= 0) & (to < groups)
-                e_dst = (1 - side_) * 3 * views + 2 * row_ + core
-                start(valid, copy(e, e_dst, slot, (2 * to + side, view)))
-                slot += 1
-            if not is_own and not (first and d_side == 0):
-                start(None, copy(e, e, slot, sibling))
-                slot += 1
-        if not last:
-            for row_ in (0, 1):
-                for base, condition in ((0, has_below), (3 * views, has_above)):
-                    e = base + 2 * row_ + core
-                    made = copy(e, e, slot, sibling)
-                    pl.when(condition)(arrival(e).wait_recv)
-                    start(condition, made)
-                    slot += 1
+                send_beside(stage, c, kind, 4 + 2 * kind[0] + kind[1])
+            start(stage, c, None, e, e, 8 + 2 * kind[0] + kind[1], sibling)
+
+    def spread_beside(stage, c):
+        if stage == ITERS:
+            return
+        for row_ in (0, 1):
+            for k, base, condition in ((0, 0, has_below), (1, 3 * views, has_above)):
+                e = base + 2 * row_ + core
+                pl.when(condition)(arrival(stage, c, e).wait_recv)
+                start(stage, c, condition, e, e, 12 + 2 * row_ + k, sibling)
+
+    def spread_done(stage, c):
+        first, last = stage == 0, stage == ITERS
         other = 1 - core
-        for d_side, d_row in kinds:
-            if first and d_side == 0:
-                continue
-            side_ = lax.rem(side + d_side, 2)
-            row_ = lax.rem(row + d_row, 2)
-            arrival(slot_of(side_, row_, other)).wait_recv()
-        if not last:
-            for row_ in (0, 1):
-                pl.when(has_below)(arrival(2 * row_ + other).wait_recv)
-                pl.when(has_above)(arrival(3 * views + 2 * row_ + other).wait_recv)
-        for condition, made in sent:
+        for row_ in (0, 1):
+            if not first:
+                arrival(stage, c, slot_of(side, row_, other)).wait_recv()
+            if not last:
+                arrival(stage, c, slot_of(1 - side, row_, other)).wait_recv()
+                pl.when(has_below)(arrival(stage, c, 2 * row_ + other).wait_recv)
+                pl.when(has_above)(arrival(stage, c, 3 * views + 2 * row_ + other).wait_recv)
+        for condition, where in sent[(stage, c)]:
+            made = copy_part(stage, c, *where)
             if condition is None:
                 made.wait_send()
             else:
@@ -488,152 +513,199 @@
     def stacked_up(beside):
         return jnp.concatenate([beside[:, :columns], beside[:, columns:]], axis=0)
 
-    def forward_z():
+    window_lines = window.reshape(2 * span * lines, columns)
+    mid_lines = mid.reshape(span * lines, columns)
+    logs_lines = logs.reshape(span * lines, columns)
+
+    def forward_z(c):
         def lines_of(i, carry):
-            for part in range(4):
-                y = i * 8 + 2 * part
-                one, two = along_z(window, z_fwd, y)
-                mid[pl.ds(y, span, stride=lines), :] = one
-                mid[pl.ds(y + 1, span, stride=lines), :] = two
+            for step in range(4):
+                y = c * chunk_lines + i * 8 + 2 * step
+                one, two = along_z(window_lines, z_fwd, y)
+                mid_lines[pl.ds(y, span, stride=lines), :] = one
+                mid_lines[pl.ds(y + 1, span, stride=lines), :] = two
             return carry
 
-        lax.fori_loop(0, lines // 8, lines_of, 0)
+        lax.fori_loop(0, chunk_lines // 8, lines_of, 0)
 
     def plane_pair(iteration, z):
-        rows = pl.ds(pl.multiple_of(z * lines, 2 * lines), 2 * lines)
-        blurred = along_x(mid[rows, :], x_fwd)
+        blurred = along_x(mid[pl.ds(z, 2)].reshape(2 * lines, columns), x_fwd)
         blurred = along_y(side_by_side(blurred), y_fwd)
         seen = jnp.concatenate([observed[z], observed[z + 1]], axis=1)
         back = along_y(seen / blurred, y_back)
         back = along_x(stacked_up(back), x_back)
-        there = pl.ds(pl.multiple_of((planes + z) * lines, 2 * lines), 2 * lines)
-        quot[iteration, there, :] = back
-
-    def edge(iteration, s, up):
-        start = (2 * planes if up else planes) + 2 * s
-        end = (0 if up else 3 * planes) + 2 * s
-        to = me + 2 if up else me - 2
+        quot[iteration, pl.ds(planes + z, 2)] = back.reshape(2, lines, columns)
+
+    early = CHUNKS // 2
+    steps = planes // 2
+
+    def edge(iteration, index, up, plane, count, lines_at):
+        start_plane = (2 * planes if up else planes) + plane
+        end_plane = (0 if up else 3 * planes) + plane
         way = 1 if up else 0
         return pltpu.make_async_remote_copy(
-            src_ref=quot.at[iteration, pl.ds(start * lines, 2 * lines)],
-            dst_ref=quot.at[iteration, pl.ds(end * lines, 2 * lines)],
-            send_sem=edge_sem.at[0, iteration, way, s],
-            recv_sem=edge_sem.at[1, iteration, way, s],
-            device_id=(to, view),
+            src_ref=quot.at[iteration, pl.ds(start_plane, count), lines_at],
+            dst_ref=quot.at[iteration, pl.ds(end_plane, count), lines_at],
+            send_sem=edge_sem.at[0, iteration, way, index],
+            recv_sem=edge_sem.at[1, iteration, way, index],
+            device_id=(me + 2 if up else me - 2, view),
             device_id_type=MESH,
         )
+
+    def early_edge(iteration, s, up):
+        return edge(iteration, s, up, 2 * s, 2, pl.ds(0, early * chunk_lines))
+
+    def late_edge(iteration, c, up):
+        return edge(iteration, steps + c - early, up, 0, planes, chunk(c))
 
     def middle(iteration):
         def step(s, carry):
             plane_pair(iteration, 2 * s)
             plane_pair(iteration, planes + 2 * s)
-            pl.when(has_below)(edge(iteration, s, False).start)
-            pl.when(has_above)(edge(iteration, s, True).start)
+            pl.when(has_below)(early_edge(iteration, s, False).start)
+            pl.when(has_above)(early_edge(iteration, s, True).start)
             return carry
 
-        lax.fori_loop(0, planes // 2, step, 0)
-
+        lax.fori_loop(0, steps, step, 0)
+        for c in range(early, CHUNKS):
+            pl.when(has_below)(late_edge(iteration, c, False).start)
+            pl.when(has_above)(late_edge(iteration, c, True).start)
+
+    def edges_arrived(iteration, c):
         def finish(s, carry):
-            @pl.when(has_below)
-            def _():
-                edge(iteration, s, False).wait_send()
-                edge(iteration, s, True).wait_recv()
-
-            @pl.when(has_above)
-            def _():
-                edge(iteration, s, True).wait_send()
-                edge(iteration, s, False).wait_recv()
-
+            pl.when(has_above)(early_edge(iteration, s, False).wait_recv)
+            pl.when(has_below)(early_edge(iteration, s, True).wait_recv)
             return carry
 
-        lax.fori_loop(0, planes // 2, finish, 0)
-
-    def backward_z(iteration):
-        source = quot.at[iteration]
+        if c == 0:
+            lax.fori_loop(0, steps, finish, 0)
+        if c >= early:
+            pl.when(has_above)(late_edge(iteration, c, False).wait_recv)
+            pl.when(has_below)(late_edge(iteration, c, True).wait_recv)
+
+    def edges_sent(iteration):
+        def finish(s, carry):
+            pl.when(has_below)(early_edge(iteration, s, False).wait_send)
+            pl.when(has_above)(early_edge(iteration, s, True).wait_send)
+            return carry
+
+        lax.fori_loop(0, steps, finish, 0)
+        for c in range(early, CHUNKS):
+            pl.when(has_below)(late_edge(iteration, c, False).wait_send)
+            pl.when(has_above)(late_edge(iteration, c, True).wait_send)
+
+    def backward_z(iteration, c):
+        source = quot.at[iteration].reshape(2 * span * lines, columns)
 
         def lines_of(i, carry):
-            for part in range(4):
-                y = i * 8 + 2 * part
+            for part_ in range(4):
+                y = c * chunk_lines + i * 8 + 2 * part_
                 for step, back in enumerate(along_z(source, z_back, y)):
                     value = jnp.log(back) - (log_z[...] + log_xy[pl.ds(y + step, 1), :])
-                    logs[pl.ds(y + step, span, stride=lines), :] = weight[...] * value
+                    logs_lines[pl.ds(y + step, span, stride=lines), :] = weight[...] * value
             return carry
 
-        lax.fori_loop(0, lines // 8, lines_of, 0)
-
-    def block_rows(b):
-        return pl.ds(pl.multiple_of(b * (block * lines), block * lines), block * lines)
-
-    def reduce_and_update(iteration):
-        kinds = [(1, 1), (1, 0), (0, 1), (0, 0)]
-
-        def log_block(kind, core_):
-            side_ = lax.rem(side + kind[0], 2)
-            row_ = lax.rem(row + kind[1], 2)
-            return views * side_ + 2 * row_ + core_
-
-        def to_sibling(k):
-            return pltpu.make_async_remote_copy(
-                src_ref=logs.at[block_rows(log_block(kinds[k], 1 - core))],
-                dst_ref=pair_sum.at[iteration, k],
-                send_sem=pair_sem.at[0, iteration, k],
-                recv_sem=pair_sem.at[1, iteration, k],
-                device_id=sibling,
-                device_id_type=MESH,
-            )
-
-        def to_peer(k):
-            side_ = lax.rem(side + kinds[k][0], 2)
-            row_ = lax.rem(row + kinds[k][1], 2)
-            return pltpu.make_async_remote_copy(
-                src_ref=logs.at[block_rows(log_block(kinds[k], core))],
-                dst_ref=peer_sum.at[iteration, k],
-                send_sem=peer_sem.at[0, iteration, k],
-                recv_sem=peer_sem.at[1, iteration, k],
-                device_id=device(side_, 2 * row_ + core),
-                device_id_type=MESH,
-            )
-
+        lax.fori_loop(0, chunk_lines // 8, lines_of, 0)
+
+    kinds = [(1, 1), (1, 0), (0, 1), (0, 0)]
+
+    def log_block(kind, core_):
+        side_ = lax.rem(side + kind[0], 2)
+        row_ = lax.rem(row + kind[1], 2)
+        return pl.ds((views * side_ + 2 * row_ + core_) * block, block)
+
+    def to_sibling(iteration, c, k):
+        return pltpu.make_async_remote_copy(
+            src_ref=logs.at[log_block(kinds[k], 1 - core), chunk(c)],
+            dst_ref=pair_sum.at[iteration, k, :, chunk(c)],
+            send_sem=pair_sem.at[0, iteration, c, k],
+            recv_sem=pair_sem.at[1, iteration, c, k],
+            device_id=sibling,
+            device_id_type=MESH,
+        )
+
+    def to_peer(iteration, c, k):
+        side_ = lax.rem(side + kinds[k][0], 2)
+        row_ = lax.rem(row + kinds[k][1], 2)
+        return pltpu.make_async_remote_copy(
+            src_ref=logs.at[log_block(kinds[k], core), chunk(c)],
+            dst_ref=peer_sum.at[iteration, k, :, chunk(c)],
+            send_sem=peer_sem.at[0, iteration, c, k],
+            recv_sem=peer_sem.at[1, iteration, c, k],
+            device_id=device(side_, 2 * row_ + core),
+            device_id_type=MESH,
+        )
+
+    def correct(iteration, c):
+        edges_arrived(iteration, c)
+        backward_z(iteration, c)
         for k in range(4):
-            to_sibling(k).start()
+            to_sibling(iteration, c, k).start()
+
+    def reduce_pair(iteration, c):
         for k in range(4):
-            to_sibling(k).wait_recv()
-            mine = block_rows(log_block(kinds[k], core))
-            logs[mine, :] = logs[mine, :] + pair_sum[iteration, k]
+            to_sibling(iteration, c, k).wait_recv()
+            mine = log_block(kinds[k], core)
+            logs[mine, chunk(c)] = logs[mine, chunk(c)] + pair_sum[iteration, k, :, chunk(c)]
             if k < 3:
-                to_peer(k).start()
+                to_peer(iteration, c, k).start()
+
+    def update(iteration, c):
         for k in (1, 2, 0):
-            to_peer(k).wait_recv()
+            to_peer(iteration, c, k).wait_recv()
         count = jnp.sum(cover_ref[...], axis=0, keepdims=True)
-        mine = block_rows(views * side + view)
-        total = logs[mine, :] + peer_sum[iteration, 0] + peer_sum[iteration, 1] + peer_sum[iteration, 2]
-        here = window_rows(views + views * side + view)
-        window[here, :] = window[here, :] * jnp.exp(total / count)
+        total = logs[log_block((0, 0), core), chunk(c)]
+        for k in range(3):
+            total = total + peer_sum[iteration, k, :, chunk(c)]
+        here = pl.ds(own * block, block)
+        window[here, chunk(c)] = window[here, chunk(c)] * jnp.exp(total / count[None])
+        spread_own(iteration + 1, c)
+
+    def sums_sent(iteration, c):
         for k in range(4):
-            to_sibling(k).wait_send()
+            to_sibling(iteration, c, k).wait_send()
         for k in range(3):
-            to_peer(k).wait_send()
-
+            to_peer(iteration, c, k).wait_send()
+
+    def settle(stage, c):
+        spread_done(stage, c)
+        if stage < ITERS:
+            forward_z(c)
+        else:
+            out_ref[:, chunk(c)] = window[own_planes, chunk(c)]
+
+    def pipeline(stages):
+        for t in range(CHUNKS + len(stages) - 1):
+            for lag, stage in enumerate(stages):
+                if 0 <= t - lag < CHUNKS:
+                    stage(t - lag)
+
+    zero = jnp.zeros((planes, lines, columns), F32)
+
+    @pl.when(group == 0)
+    def _():
+        window[:planes] = zero
+        for iteration in range(ITERS):
+            quot[iteration, :planes] = zero
+
+    @pl.when(group == groups - 1)
+    def _():
+        window[3 * planes :] = zero
+        for iteration in range(ITERS):
+            quot[iteration, 3 * planes :] = zero
+
+    for c in range(CHUNKS):
+        spread_own(0, c)
     turn()
     start_views()
-
-    @pl.when(group == 0)
-    def _():
-        below = pl.ds(0, planes * lines)
-        window[below, :] = jnp.zeros((planes * lines, columns), F32)
-        for iteration in range(ITERS):
-            quot[iteration, below, :] = jnp.zeros((planes * lines, columns), F32)
-
-    @pl.when(group == groups - 1)
-    def _():
-        above = pl.ds(3 * planes * lines, planes * lines)
-        window[above, :] = jnp.zeros((planes * lines, columns), F32)
-        for iteration in range(ITERS):
-            quot[iteration, above, :] = jnp.zeros((planes * lines, columns), F32)
-
-    share(0, True, False)
     prepare()
-    forward_z()
+    pipeline(
+        [
+            functools.partial(spread_group, 0),
+            functools.partial(spread_beside, 0),
+            functools.partial(settle, 0),
+        ]
+    )
     cover_copy.wait_send()
     remote(cover.at[1 - side], cover.at[1 - side], cover_sem, 0, sibling).wait_recv()
     which = takes_lateral * views + view
@@ -641,13 +713,20 @@
     weight[planes:, :] = jnp.broadcast_to(cover[1, pl.ds(which, 1), :], (planes, columns))
     finish_views()
     for iteration in range(ITERS):
-        if iteration > 0:
-            forward_z()
         middle(iteration)
-        backward_z(iteration)
-        reduce_and_update(iteration)
-        share(iteration + 1, False, iteration == ITERS - 1)
-    out_ref[...] = window[own_rows, :]
+        pipeline(
+            [
+                functools.partial(correct, iteration),
+                functools.partial(reduce_pair, iteration),
+                functools.partial(update, iteration),
+                functools.partial(spread_group, iteration + 1),
+                functools.partial(spread_beside, iteration + 1),
+                functools.partial(settle, iteration + 1),
+            ]
+        )
+        edges_sent(iteration)
+        for c in range(CHUNKS):
+            sums_sent(iteration, c)
 
 
 def joint(estimate, axial_views, lateral_views, psf_axial, psf_lateral, coverage):
@@ -657,7 +736,7 @@
     slab = columns // owners
     span = 2 * planes
     depth = owners * planes
-    block_rows = planes // views * lines
+    block = planes // views
     takes_lateral = (lax.axis_index("owner") + lax.axis_index("view")) % 2 == 1
     psf = jnp.where(takes_lateral, psf_lateral[0], psf_axial[0])
     psf = psf / jnp.sum(psf, axis=-1, keepdims=True)
@@ -666,18 +745,18 @@
     dma = pltpu.SemaphoreType.DMA
     result = pl.pallas_call(
         functools.partial(joint_kernel, owners, views, planes, lines, columns),
-        out_shape=jax.ShapeDtypeStruct((planes * lines, columns), F32),
+        out_shape=jax.ShapeDtypeStruct((planes, lines, columns), F32),
         in_specs=[pl.BlockSpec(memory_space=pltpu.SMEM)] + [vmem] * 4,
         out_specs=vmem,
         scratch_shapes=[
-            pltpu.VMEM((2 * span * lines, columns), F32),
+            pltpu.VMEM((2 * span, lines, columns), F32),
             pltpu.VMEM((span, lines, columns), F32),
             pltpu.VMEM((depth, slab, lines), F32),
-            pltpu.VMEM((span * lines, columns), F32),
-            pltpu.VMEM((ITERS, 2 * span * lines, columns), F32),
-            pltpu.VMEM((span * lines, columns), F32),
-            pltpu.VMEM((ITERS, 4, block_rows, columns), F32),
-            pltpu.VMEM((ITERS, 3, block_rows, columns), F32),
+            pltpu.VMEM((span, lines, columns), F32),
+            pltpu.VMEM((ITERS, 2 * span, lines, columns), F32),
+            pltpu.VMEM((span, lines, columns), F32),
+            pltpu.VMEM((ITERS, 4, block, lines, columns), F32),
+            pltpu.VMEM((ITERS, 3, block, lines, columns), F32),
             pltpu.VMEM((2,) + cover.shape, F32),
             pltpu.VMEM((2 * columns, 2 * columns), BF16),
             pltpu.VMEM((2 * columns, 2 * columns), BF16),
@@ -691,22 +770,22 @@
             dma((2, 1)),
             dma((2, 1)),
             dma((2, owners)),
-            dma((2, ITERS, 2, planes // 2)),
-            dma((2, ITERS + 1, 4 * views)),
-            dma((2, ITERS, 4)),
-            dma((2, ITERS, 4)),
+            dma((2, ITERS, 2, planes // 2 + CHUNKS)),
+            dma((2, ITERS + 1, CHUNKS, 4 * views)),
+            dma((2, ITERS, CHUNKS, 4)),
+            dma((2, ITERS, CHUNKS, 4)),
         ],
         compiler_params=pltpu.CompilerParams(
             collective_id=0, has_side_effects=True, vmem_limit_bytes=48 * 1024 * 1024
         ),
     )(
         psf.reshape(-1),
-        estimate.reshape(planes * lines, columns),
+        estimate,
         axial_views[0],
         lateral_views[0],
         cover,
     )
-    return result.reshape(planes, lines, columns)
+    return result
 
 
 def chosen(estimate, axial_views, lateral_views, psf_axial, psf_lateral, coverage):
@@ -726,6 +805,7 @@
         and planes % views == 0
         and rim <= planes
         and columns // owners % 8 == 0
+        and lines % (8 * CHUNKS) == 0
     )
     body = joint if fits else local
     return body(estimate, axial_views, lateral_views, psf_axial, psf_lateral, coverage)

time: 194 us -> 152 us (0.78)
  Pallas kernels: 187 us -> 145 us
    pallas_call x1, Pallas kernels: 187 us -> 145 us  [joint(): pl.pallas_call(functools.partial(joint_kernel, owners, views, planes, lin...]
where the time goes in v2:
time: 152 us
  Pallas kernels  145 us (95%)
  local copies, waits for them, and re-layouts  6.42 us (4%)
    pallas_call x1, Pallas kernels, joint(): pl.pallas_call(functools.partial(joint_kernel, owners, views, planes, lin...  145 us
    unnamed x13, local copies, waits for them, and re-layouts  5.95 us

profile of v2, /device:TPU:0, one launch (start us, length us, event | category | flops | bytes accessed | tf_op | source)
XLA Modules:
  0.0 151.9 jit_solution(15235578815216308386)
XLA Ops:
  0.0 0.0 copy-start.3
  0.0 0.7 copy-done.3
  0.7 0.0 copy-start.4
  0.7 0.0 copy-start.5
  0.7 0.1 copy.7
  0.8 0.6 copy-done.4
  1.4 0.0 copy-done.5
  1.4 0.1 fusion
  1.5 0.1 select_n.23
  1.6 0.1 div.11
  1.6 0.1 div.12
  1.7 0.1 broadcast_in_dim.4
  1.8 0.1 reshape.13.cover_ref
  1.9 0.0 copy-start
  1.9 1.2 copy-done
  3.1 0.0 copy-start.1
  3.1 1.2 copy-done.1
  4.4 0.0 copy-start.2
  4.4 1.2 copy-done.2
  5.6 145.4 %shard_map.64 = f32[16,128,128]{2,1,0:T(8,128)S(1)} custom-call(f32[99]{0:T(128)S(1)} %div.13.psf_ref, f32[16,128,128]{2,1,0:T(8,128)S(1)} %copy-done, f32[16,128,128]{2,1,0:T(8,128)S(1)} %bitcast.6, f32[16,128,128]{2,1,0:T(8,128)S(1)} %bitcast.7, f32[8,128]{1,0:T(8,128)S(1)} %reshape.13.cover_ref), custom_call_target="tpu_custom_call" | custom-call | tf_op jit(solution)/shard_map/pallas_call | solution.py:746
  151.0 1.0 copy.9
  (2 shorter events, 0.0 us)
Async XLA Ops:
  0.0 0.7 copy-start.3
  0.7 0.7 copy-start.4
  0.7 0.7 copy-start.5
  1.9 1.2 copy-start
  3.1 1.2 copy-start.1
  4.4 1.2 copy-start.2

commit v3 on v2

--- a/solution.py
+++ b/solution.py
@@ -169,7 +169,8 @@
 F32 = jnp.float32
 BF16 = jnp.bfloat16
 MESH = pl.DeviceIdType.MESH
-CHUNKS = 4
+CHUNKS = 8
+PARTS = 4
 
 
 def split_bf16(values):
@@ -196,6 +197,7 @@
     out_ref,
     window,
     observed,
+    lateral,
     turned,
     mid,
     quot,
@@ -219,6 +221,7 @@
     share_sem,
     pair_sem,
     peer_sem,
+    local_sem,
 ):
     taps = psf_ref.shape[0] // 3
     rim = (taps - 1) // 2
@@ -257,8 +260,26 @@
                 device_id_type=MESH,
             )
     own_planes = pl.ds(planes + planes * side, planes)
-    window[own_planes] = estimate_ref[...]
+    estimate_in = pltpu.make_async_copy(estimate_ref, window.at[own_planes], local_sem.at[0])
+    lateral_in = pltpu.make_async_copy(lateral_ref, lateral, local_sem.at[1])
+    estimate_in.start()
+    lateral_in.start()
     cover[pl.ds(side, 1)] = cover_ref[...][None]
+
+    def clear(base):
+        def plane(z, carry):
+            zero = jnp.zeros((lines, columns), F32)
+            window[base + z] = zero
+            for iteration in range(ITERS):
+                quot[iteration, base + z] = zero
+            return carry
+
+        lax.fori_loop(0, planes, plane, 0)
+
+    pl.when(group == 0)(lambda: clear(0))
+    pl.when(group == groups - 1)(lambda: clear(3 * planes))
+
+    estimate_in.wait()
     pl.semaphore_wait(barrier, owners - 1 + 2 * (views - 1))
 
     def remote(src, dst, sems, index, target):
@@ -419,70 +440,104 @@
     cover_copy.start()
     axial_target = device(core, view)
     axial_mine = pl.ds(side * planes, planes)
-    axial_copy = remote(axial_ref, observed.at[axial_mine], axial_sem, 0, axial_target)
-
-    def lateral_copy(to):
+    depth = planes // PARTS
+    axial_in = pltpu.make_async_copy(axial_ref, observed.at[axial_mine], local_sem.at[2])
+
+    def axial_copy(q):
+        return remote(
+            axial_ref.at[pl.ds(q * depth, depth)],
+            observed.at[pl.ds(side * planes + q * depth, depth)],
+            axial_sem,
+            q,
+            axial_target,
+        )
+
+    def axial_arrival(q):
+        theirs = observed.at[pl.ds((1 - side) * planes + q * depth, depth)]
+        return remote(theirs, theirs, axial_sem, q, sibling)
+
+    def lateral_copy(to, q, half):
+        plane = half * planes + q * depth
         return pltpu.make_async_remote_copy(
-            src_ref=turned.at[pl.ds(to * span, span)],
-            dst_ref=observed.at[:, pl.ds(me * slab, slab), :],
-            send_sem=lateral_sem.at[0, to],
-            recv_sem=lateral_sem.at[1, me],
+            src_ref=turned.at[pl.ds(to * span + plane, depth)],
+            dst_ref=observed.at[pl.ds(plane, depth), pl.ds(me * slab, slab), :],
+            send_sem=lateral_sem.at[0, to, q, half],
+            recv_sem=lateral_sem.at[1, me, q, half],
             device_id=(2 * to + 1 - core, view),
             device_id_type=MESH,
         )
 
-    def lateral_arrival(source):
+    def lateral_arrival(source, q, half):
+        there = observed.at[pl.ds(half * planes + q * depth, depth), pl.ds(source * slab, slab), :]
         return pltpu.make_async_remote_copy(
-            src_ref=observed.at[:, pl.ds(source * slab, slab), :],
-            dst_ref=observed.at[:, pl.ds(source * slab, slab), :],
-            send_sem=lateral_sem.at[0, 0],
-            recv_sem=lateral_sem.at[1, source],
+            src_ref=there,
+            dst_ref=there,
+            send_sem=lateral_sem.at[0, 0, q, half],
+            recv_sem=lateral_sem.at[1, source, q, half],
             device_id=sibling,
             device_id_type=MESH,
         )
 
     def turn():
+        lateral_in.wait()
         for x in range(slab):
-            turned[:, x, :] = lateral_ref[x].T
-
-    def start_views():
+            turned[:, x, :] = lateral[x].T
+
+    def each_lateral(act):
+        for q in range(PARTS):
+            for to in range(groups):
+
+                @pl.when((takes_lateral == 0) | (to != group))
+                def _():
+                    act(lateral_copy(to, q, 0))
+                    act(lateral_copy(to, q, 1))
+
+    def start_axial():
         @pl.when(takes_lateral == 1)
         def _():
-            axial_copy.start()
-
-        for to in range(groups):
-
-            @pl.when((takes_lateral == 0) | (to != group))
-            def _():
-                lateral_copy(to).start()
-
-    def finish_views():
+            for q in range(PARTS):
+                axial_copy(q).start()
+
+        @pl.when(takes_lateral == 0)
+        def _():
+            axial_in.start()
+
+    def start_lateral():
+        each_lateral(lambda copy: copy.start())
+
         @pl.when(takes_lateral == 1)
         def _():
             observed[:, pl.ds(pl.multiple_of(me * slab, slab), slab), :] = turned[
                 pl.ds(group * span, span)
             ]
-            axial_copy.wait_send()
-            for step in range(1, owners):
-                lateral_arrival(lax.rem(me + step, owners)).wait_recv()
-
-            def flip(z, carry):
-                observed[z] = observed[z].T
-                return carry
-
-            lax.fori_loop(0, span, flip, 0)
+
+    def views_arrived(q):
+        @pl.when(takes_lateral == 1)
+        def _():
+            for half in (0, 1):
+                for step in range(1, owners):
+                    lateral_arrival(lax.rem(me + step, owners), q, half).wait_recv()
+
+                def flip(z, carry):
+                    observed[z] = observed[z].T
+                    return carry
+
+                first_plane = half * planes + q * depth
+                lax.fori_loop(first_plane, first_plane + depth, flip, 0)
 
         @pl.when(takes_lateral == 0)
         def _():
-            observed[axial_mine] = axial_ref[...]
-            theirs = observed.at[pl.ds((1 - side) * planes, planes)]
-            remote(theirs, theirs, axial_sem, 0, sibling).wait_recv()
-
-        for to in range(groups):
-
-            @pl.when((takes_lateral == 0) | (to != group))
-            def _():
-                lateral_copy(to).wait_send()
+            if q == 0:
+                axial_in.wait()
+            axial_arrival(q).wait_recv()
+
+    def views_sent():
+        each_lateral(lambda copy: copy.wait_send())
+
+        @pl.when(takes_lateral == 1)
+        def _():
+            for q in range(PARTS):
+                axial_copy(q).wait_send()
 
     def along_z(source, matrix, y):
         both = jnp.concatenate(
@@ -566,7 +621,12 @@
             pl.when(has_above)(early_edge(iteration, s, True).start)
             return carry
 
-        lax.fori_loop(0, steps, step, 0)
+        if iteration == 0:
+            for q in range(PARTS):
+                views_arrived(q)
+                lax.fori_loop(q * (steps // PARTS), (q + 1) * (steps // PARTS), step, 0)
+        else:
+            lax.fori_loop(0, steps, step, 0)
         for c in range(early, CHUNKS):
             pl.when(has_below)(late_edge(iteration, c, False).start)
             pl.when(has_above)(late_edge(iteration, c, True).start)
@@ -680,24 +740,11 @@
                 if 0 <= t - lag < CHUNKS:
                     stage(t - lag)
 
-    zero = jnp.zeros((planes, lines, columns), F32)
-
-    @pl.when(group == 0)
-    def _():
-        window[:planes] = zero
-        for iteration in range(ITERS):
-            quot[iteration, :planes] = zero
-
-    @pl.when(group == groups - 1)
-    def _():
-        window[3 * planes :] = zero
-        for iteration in range(ITERS):
-            quot[iteration, 3 * planes :] = zero
-
     for c in range(CHUNKS):
         spread_own(0, c)
+    start_axial()
     turn()
-    start_views()
+    start_lateral()
     prepare()
     pipeline(
         [
@@ -711,7 +758,6 @@
     which = takes_lateral * views + view
     weight[:planes, :] = jnp.broadcast_to(cover[0, pl.ds(which, 1), :], (planes, columns))
     weight[planes:, :] = jnp.broadcast_to(cover[1, pl.ds(which, 1), :], (planes, columns))
-    finish_views()
     for iteration in range(ITERS):
         middle(iteration)
         pipeline(
@@ -727,6 +773,7 @@
         edges_sent(iteration)
         for c in range(CHUNKS):
             sums_sent(iteration, c)
+    views_sent()
 
 
 def joint(estimate, axial_views, lateral_views, psf_axial, psf_lateral, coverage):
@@ -742,15 +789,17 @@
     psf = psf / jnp.sum(psf, axis=-1, keepdims=True)
     cover = jnp.repeat(coverage[0].astype(F32).T, columns // coverage.shape[1], axis=1)
     vmem = pl.BlockSpec(memory_space=pltpu.VMEM)
+    hbm = pl.BlockSpec(memory_space=pl.ANY)
     dma = pltpu.SemaphoreType.DMA
     result = pl.pallas_call(
         functools.partial(joint_kernel, owners, views, planes, lines, columns),
         out_shape=jax.ShapeDtypeStruct((planes, lines, columns), F32),
-        in_specs=[pl.BlockSpec(memory_space=pltpu.SMEM)] + [vmem] * 4,
+        in_specs=[pl.BlockSpec(memory_space=pltpu.SMEM)] + [hbm] * 3 + [vmem],
         out_specs=vmem,
         scratch_shapes=[
             pltpu.VMEM((2 * span, lines, columns), F32),
             pltpu.VMEM((span, lines, columns), F32),
+            pltpu.VMEM((slab, lines, depth), F32),
             pltpu.VMEM((depth, slab, lines), F32),
             pltpu.VMEM((span, lines, columns), F32),
             pltpu.VMEM((ITERS, 2 * span, lines, columns), F32),
@@ -768,12 +817,13 @@
             pltpu.VMEM((span, columns), F32),
             pltpu.VMEM((span, columns), F32),
             dma((2, 1)),
-            dma((2, 1)),
-            dma((2, owners)),
+            dma((2, PARTS)),
+            dma((2, owners, PARTS, 2)),
             dma((2, ITERS, 2, planes // 2 + CHUNKS)),
             dma((2, ITERS + 1, CHUNKS, 4 * views)),
             dma((2, ITERS, CHUNKS, 4)),
             dma((2, ITERS, CHUNKS, 4)),
+            dma((3,)),
         ],
         compiler_params=pltpu.CompilerParams(
             collective_id=0, has_side_effects=True, vmem_limit_bytes=48 * 1024 * 1024
@@ -803,6 +853,7 @@
         and views == 4
         and owners % 2 == 0
         and planes % views == 0
+        and planes % (2 * PARTS) == 0
         and rim <= planes
         and columns // owners % 8 == 0
         and lines % (8 * CHUNKS) == 0

time: 152 us -> 172 us (1.13)
  Pallas kernels: 145 us -> 165 us
    pallas_call x1, Pallas kernels: 145 us -> 165 us  [joint(): pl.pallas_call(functools.partial(joint_kernel, owners, views, planes, lin...]
where the time goes in v3:
time: 172 us
  Pallas kernels  165 us (96%)
  local copies, waits for them, and re-layouts  6.42 us (4%)
    pallas_call x1, Pallas kernels, joint(): pl.pallas_call(functools.partial(joint_kernel, owners, views, planes, lin...  165 us
    unnamed x13, local copies, waits for them, and re-layouts  5.95 us

profile of v3, /device:TPU:0, one launch (start us, length us, event | category | flops | bytes accessed | tf_op | source)
XLA Modules:
  0.0 171.7 jit_solution(2671814747493577435)
XLA Ops:
  0.0 0.0 copy-start.3
  0.0 0.7 copy-done.3
  0.7 0.0 copy-start.4
  0.7 0.0 copy-start.5
  0.7 0.1 copy.7
  0.8 0.6 copy-done.4
  1.4 0.0 copy-done.5
  1.4 0.1 fusion
  1.5 0.1 select_n.23
  1.6 0.1 div.11
  1.6 0.1 div.12
  1.7 0.1 broadcast_in_dim.4
  1.8 0.1 reshape.13.cover_ref
  1.9 0.0 copy-start
  1.9 1.2 copy-done
  3.1 0.0 copy-start.1
  3.1 1.2 copy-done.1
  4.4 0.0 copy-start.2
  4.4 1.2 copy-done.2
  5.6 165.1 %shard_map.64 = f32[16,128,128]{2,1,0:T(8,128)S(1)} custom-call(f32[99]{0:T(128)S(1)} %div.13.psf_ref, f32[16,128,128]{2,1,0:T(8,128)S(1)} %copy-done, f32[16,128,128]{2,1,0:T(8,128)S(1)} %bitcast.6, f32[16,128,128]{2,1,0:T(8,128)S(1)} %bitcast.7, f32[8,128]{1,0:T(8,128)S(1)} %reshape.13.cover_ref), custom_call_target="tpu_custom_call" | custom-call | tf_op jit(solution)/shard_map/pallas_call | solution.py:794
  170.7 1.0 copy.9
  (2 shorter events, 0.0 us)
Async XLA Ops:
  0.0 0.7 copy-start.3
  0.7 0.7 copy-start.4
  0.7 0.7 copy-start.5
  1.9 1.2 copy-start
  3.1 1.2 copy-start.1
  4.4 1.2 copy-start.2

commit v4 on v3

--- a/solution.py
+++ b/solution.py
@@ -169,8 +169,8 @@
 F32 = jnp.float32
 BF16 = jnp.bfloat16
 MESH = pl.DeviceIdType.MESH
-CHUNKS = 8
-PARTS = 4
+CHUNKS = 4
+PARTS = 2
 
 
 def split_bf16(values):
@@ -271,7 +271,7 @@
             zero = jnp.zeros((lines, columns), F32)
             window[base + z] = zero
             for iteration in range(ITERS):
-                quot[iteration, base + z] = zero
+                quot[iteration * 2 * span + base + z] = zero
             return carry
 
         lax.fori_loop(0, planes, plane, 0)
@@ -293,7 +293,7 @@
         )
 
     def chunk(c):
-        return pl.ds(c * chunk_lines, chunk_lines)
+        return pl.ds(pl.multiple_of(c * chunk_lines, chunk_lines), chunk_lines)
 
     def part(e, c):
         return window.at[pl.ds(e * block, block), chunk(c)]
@@ -314,88 +314,73 @@
     def arrival(stage, c, e):
         return copy_part(stage, c, e, e, 0, sibling)
 
-    sent = {}
-
-    def start(stage, c, condition, *where):
-        made = copy_part(stage, c, *where)
-        if condition is None:
-            made.start()
-        else:
-            pl.when(condition)(made.start)
-        sent.setdefault((stage, c), []).append((condition, where))
-
     own = slot_of(side, row, core)
     row_peer = device(side, 2 * (1 - row) + core)
     side_peer = device(1 - side, view)
     far_peer = device(1 - side, 2 * (1 - row) + core)
+    other = 1 - core
+    yes = group >= 0
 
     def block_of(kind):
         side_ = lax.rem(side + kind[0], 2)
         row_ = lax.rem(row + kind[1], 2)
-        return side_, row_, slot_of(side_, row_, core)
-
-    def send_beside(stage, c, kind, slot):
-        side_, row_, e = block_of(kind)
+        return side_, slot_of(side_, row_, core)
+
+    def beside(more, kind):
+        side_, e = block_of(kind)
         to = group + 2 * side_ - 1
-        valid = (to >= 0) & (to < groups)
-        e_dst = (1 - side_) * 3 * views + 2 * row_ + core
-        start(stage, c, valid, e, e_dst, slot, (2 * to + side, view))
-
-    def spread_own(stage, c):
-        first, last = stage == 0, stage == ITERS
-        if not last:
-            start(stage, c, None, own, own, 0, side_peer)
-        if not first:
-            start(stage, c, None, own, own, 1, row_peer)
-            start(stage, c, None, own, own, 2, sibling)
-        if not first and not last:
-            start(stage, c, None, own, own, 3, far_peer)
-        if not last:
-            send_beside(stage, c, (0, 0), 4)
+        valid = (to >= 0) & (to < groups) & more
+        e_dst = e + (1 - 3 * side_) * views + (1 - side_) * views
+        return valid, e, e_dst, 4 + 2 * kind[0] + kind[1], (2 * to + side, view)
+
+    def plan(first, more):
         if first:
-            send_beside(stage, c, (0, 1), 5)
-
-    def spread_group(stage, c):
-        first, last = stage == 0, stage == ITERS
-        kinds = [(0, 1), (1, 0), (1, 1)]
-        if first:
-            kinds = kinds[1:]
-        if last:
-            kinds = kinds[:1]
-        for kind in kinds:
-            e = block_of(kind)[2]
-            arrival(stage, c, e).wait_recv()
+            at_once = [(yes, own, own, 0, side_peer), beside(yes, (0, 0)), beside(yes, (0, 1))]
+        else:
+            at_once = [
+                (more, own, own, 0, side_peer),
+                (yes, own, own, 1, row_peer),
+                (yes, own, own, 2, sibling),
+                (more, own, own, 3, far_peer),
+                beside(more, (0, 0)),
+            ]
+        group_steps = []
+        for kind in [(1, 0), (1, 1)] if first else [(0, 1), (1, 0), (1, 1)]:
+            e = block_of(kind)[1]
+            when = yes if kind == (0, 1) else more
+            onward = [beside(more, kind), (when, e, e, 8 + 2 * kind[0] + kind[1], sibling)]
             if first and kind == (1, 0):
-                start(stage, c, None, e, e, 3, row_peer)
-            if not last:
-                send_beside(stage, c, kind, 4 + 2 * kind[0] + kind[1])
-            start(stage, c, None, e, e, 8 + 2 * kind[0] + kind[1], sibling)
-
-    def spread_beside(stage, c):
-        if stage == ITERS:
-            return
+                onward.append((yes, e, e, 3, row_peer))
+            group_steps.append((when, e, onward))
+        beside_steps = []
+        rest = []
         for row_ in (0, 1):
             for k, base, condition in ((0, 0, has_below), (1, 3 * views, has_above)):
                 e = base + 2 * row_ + core
-                pl.when(condition)(arrival(stage, c, e).wait_recv)
-                start(stage, c, condition, e, e, 12 + 2 * row_ + k, sibling)
-
-    def spread_done(stage, c):
-        first, last = stage == 0, stage == ITERS
-        other = 1 - core
-        for row_ in (0, 1):
+                onward = [(condition & more, e, e, 12 + 2 * row_ + k, sibling)]
+                beside_steps.append((condition & more, e, onward))
+                rest.append((condition & more, base + 2 * row_ + other))
             if not first:
-                arrival(stage, c, slot_of(side, row_, other)).wait_recv()
-            if not last:
-                arrival(stage, c, slot_of(1 - side, row_, other)).wait_recv()
-                pl.when(has_below)(arrival(stage, c, 2 * row_ + other).wait_recv)
-                pl.when(has_above)(arrival(stage, c, 3 * views + 2 * row_ + other).wait_recv)
-        for condition, where in sent[(stage, c)]:
-            made = copy_part(stage, c, *where)
-            if condition is None:
-                made.wait_send()
-            else:
-                pl.when(condition)(made.wait_send)
+                rest.append((yes, slot_of(side, row_, other)))
+            rest.append((more, slot_of(1 - side, row_, other)))
+        return at_once, group_steps, beside_steps, rest
+
+    def start_all(stage, c, sends):
+        for condition, *where in sends:
+            pl.when(condition)(copy_part(stage, c, *where).start)
+
+    def send_on(stage, c, steps_):
+        for condition, e, onward in steps_:
+            pl.when(condition)(arrival(stage, c, e).wait_recv)
+            start_all(stage, c, onward)
+
+    def spread_done(stage, c, made):
+        at_once, group_steps, beside_steps, rest = made
+        for condition, e in rest:
+            pl.when(condition)(arrival(stage, c, e).wait_recv)
+        onwards = [onward for _, _, onward in group_steps + beside_steps]
+        for condition, *where in sum(onwards, at_once):
+            pl.when(condition)(copy_part(stage, c, *where).wait_send)
 
     def toeplitz(axis, shape, offset, flip):
         first = lax.broadcasted_iota(jnp.int32, shape, 0)
@@ -484,13 +469,17 @@
             turned[:, x, :] = lateral[x].T
 
     def each_lateral(act):
-        for q in range(PARTS):
-            for to in range(groups):
-
-                @pl.when((takes_lateral == 0) | (to != group))
-                def _():
-                    act(lateral_copy(to, q, 0))
-                    act(lateral_copy(to, q, 1))
+        def one(i, carry):
+            q, to = i // groups, lax.rem(i, groups)
+
+            @pl.when((takes_lateral == 0) | (to != group))
+            def _():
+                act(lateral_copy(to, q, 0))
+                act(lateral_copy(to, q, 1))
+
+            return carry
+
+        lax.fori_loop(0, PARTS * groups, one, 0)
 
     def start_axial():
         @pl.when(takes_lateral == 1)
@@ -514,21 +503,25 @@
     def views_arrived(q):
         @pl.when(takes_lateral == 1)
         def _():
-            for half in (0, 1):
-                for step in range(1, owners):
-                    lateral_arrival(lax.rem(me + step, owners), q, half).wait_recv()
-
-                def flip(z, carry):
-                    observed[z] = observed[z].T
-                    return carry
-
-                first_plane = half * planes + q * depth
-                lax.fori_loop(first_plane, first_plane + depth, flip, 0)
+            def from_owner(step, carry):
+                source = lax.rem(me + step, owners)
+                lateral_arrival(source, q, 0).wait_recv()
+                lateral_arrival(source, q, 1).wait_recv()
+                return carry
+
+            lax.fori_loop(1, owners, from_owner, 0)
+
+            def flip(k, carry):
+                z = q * depth + k
+                observed[z] = observed[z].T
+                observed[planes + z] = observed[planes + z].T
+                return carry
+
+            lax.fori_loop(0, depth, flip, 0)
 
         @pl.when(takes_lateral == 0)
         def _():
-            if q == 0:
-                axial_in.wait()
+            pl.when(q == 0)(axial_in.wait)
             axial_arrival(q).wait_recv()
 
     def views_sent():
@@ -539,11 +532,11 @@
             for q in range(PARTS):
                 axial_copy(q).wait_send()
 
-    def along_z(source, matrix, y):
+    def along_z(source, matrix, y, first_row=0):
         both = jnp.concatenate(
             [
-                source[pl.ds(y, 2 * span, stride=lines), :],
-                source[pl.ds(y + 1, 2 * span, stride=lines), :],
+                source[pl.ds(first_row + y, 2 * span, stride=lines), :],
+                source[pl.ds(first_row + y + 1, 2 * span, stride=lines), :],
             ],
             axis=1,
         )
@@ -571,6 +564,7 @@
     window_lines = window.reshape(2 * span * lines, columns)
     mid_lines = mid.reshape(span * lines, columns)
     logs_lines = logs.reshape(span * lines, columns)
+    quot_lines = quot.reshape(ITERS * 2 * span * lines, columns)
 
     def forward_z(c):
         def lines_of(i, carry):
@@ -589,7 +583,7 @@
         seen = jnp.concatenate([observed[z], observed[z + 1]], axis=1)
         back = along_y(seen / blurred, y_back)
         back = along_x(stacked_up(back), x_back)
-        quot[iteration, pl.ds(planes + z, 2)] = back.reshape(2, lines, columns)
+        quot[pl.ds(iteration * 2 * span + planes + z, 2)] = back.reshape(2, lines, columns)
 
     early = CHUNKS // 2
     steps = planes // 2
@@ -599,8 +593,8 @@
         end_plane = (0 if up else 3 * planes) + plane
         way = 1 if up else 0
         return pltpu.make_async_remote_copy(
-            src_ref=quot.at[iteration, pl.ds(start_plane, count), lines_at],
-            dst_ref=quot.at[iteration, pl.ds(end_plane, count), lines_at],
+            src_ref=quot.at[pl.ds(iteration * 2 * span + start_plane, count), lines_at],
+            dst_ref=quot.at[pl.ds(iteration * 2 * span + end_plane, count), lines_at],
             send_sem=edge_sem.at[0, iteration, way, index],
             recv_sem=edge_sem.at[1, iteration, way, index],
             device_id=(me + 2 if up else me - 2, view),
@@ -621,15 +615,17 @@
             pl.when(has_above)(early_edge(iteration, s, True).start)
             return carry
 
-        if iteration == 0:
-            for q in range(PARTS):
-                views_arrived(q)
-                lax.fori_loop(q * (steps // PARTS), (q + 1) * (steps // PARTS), step, 0)
-        else:
-            lax.fori_loop(0, steps, step, 0)
+        def part_of(q, carry):
+            pl.when(iteration == 0)(lambda: views_arrived(q))
+            return lax.fori_loop(q * (steps // PARTS), (q + 1) * (steps // PARTS), step, carry)
+
+        lax.fori_loop(0, PARTS, part_of, 0)
         for c in range(early, CHUNKS):
             pl.when(has_below)(late_edge(iteration, c, False).start)
             pl.when(has_above)(late_edge(iteration, c, True).start)
+
+    def run(body):
+        lax.fori_loop(0, steps, body, 0)
 
     def edges_arrived(iteration, c):
         def finish(s, carry):
@@ -637,11 +633,9 @@
             pl.when(has_below)(early_edge(iteration, s, True).wait_recv)
             return carry
 
-        if c == 0:
-            lax.fori_loop(0, steps, finish, 0)
-        if c >= early:
-            pl.when(has_above)(late_edge(iteration, c, False).wait_recv)
-            pl.when(has_below)(late_edge(iteration, c, True).wait_recv)
+        pl.when(c == 0)(lambda: run(finish))
+        pl.when((c >= early) & has_above)(lambda: late_edge(iteration, c, False).wait_recv())
+        pl.when((c >= early) & has_below)(lambda: late_edge(iteration, c, True).wait_recv())
 
     def edges_sent(iteration):
         def finish(s, carry):
@@ -655,12 +649,12 @@
             pl.when(has_above)(late_edge(iteration, c, True).wait_send)
 
     def backward_z(iteration, c):
-        source = quot.at[iteration].reshape(2 * span * lines, columns)
+        first_row = iteration * 2 * span * lines
 
         def lines_of(i, carry):
             for part_ in range(4):
                 y = c * chunk_lines + i * 8 + 2 * part_
-                for step, back in enumerate(along_z(source, z_back, y)):
+                for step, back in enumerate(along_z(quot_lines, z_back, y, first_row)):
                     value = jnp.log(back) - (log_z[...] + log_xy[pl.ds(y + step, 1), :])
                     logs_lines[pl.ds(y + step, span, stride=lines), :] = weight[...] * value
             return carry
@@ -710,7 +704,7 @@
             if k < 3:
                 to_peer(iteration, c, k).start()
 
-    def update(iteration, c):
+    def update(iteration, made, c):
         for k in (1, 2, 0):
             to_peer(iteration, c, k).wait_recv()
         count = jnp.sum(cover_ref[...], axis=0, keepdims=True)
@@ -719,7 +713,7 @@
             total = total + peer_sum[iteration, k, :, chunk(c)]
         here = pl.ds(own * block, block)
         window[here, chunk(c)] = window[here, chunk(c)] * jnp.exp(total / count[None])
-        spread_own(iteration + 1, c)
+        start_all(iteration + 1, c, made[0])
 
     def sums_sent(iteration, c):
         for k in range(4):
@@ -727,52 +721,78 @@
         for k in range(3):
             to_peer(iteration, c, k).wait_send()
 
-    def settle(stage, c):
-        spread_done(stage, c)
-        if stage < ITERS:
+    def pipeline(stages):
+        def turn_of(t, carry):
+            for lag, stage in enumerate(stages):
+                c = t - lag
+                pl.when((c >= 0) & (c < CHUNKS))(functools.partial(stage, c))
+            return carry
+
+        lax.fori_loop(0, CHUNKS + len(stages) - 1, turn_of, 0)
+
+    def initial():
+        made = plan(True, yes)
+
+        def begin(c, carry):
+            start_all(0, c, made[0])
+            return carry
+
+        lax.fori_loop(0, CHUNKS, begin, 0)
+        start_axial()
+        turn()
+        start_lateral()
+        prepare()
+
+        def settle(c):
+            spread_done(0, c, made)
             forward_z(c)
-        else:
-            out_ref[:, chunk(c)] = window[own_planes, chunk(c)]
-
-    def pipeline(stages):
-        for t in range(CHUNKS + len(stages) - 1):
-            for lag, stage in enumerate(stages):
-                if 0 <= t - lag < CHUNKS:
-                    stage(t - lag)
-
-    for c in range(CHUNKS):
-        spread_own(0, c)
-    start_axial()
-    turn()
-    start_lateral()
-    prepare()
-    pipeline(
-        [
-            functools.partial(spread_group, 0),
-            functools.partial(spread_beside, 0),
-            functools.partial(settle, 0),
-        ]
-    )
+
+        pipeline(
+            [lambda c: send_on(0, c, made[1]), lambda c: send_on(0, c, made[2]), settle]
+        )
+
+    def one_pass(iteration, carry):
+        more = iteration < ITERS - 1
+        made = plan(False, more)
+        stage = iteration + 1
+        middle(iteration)
+
+        def settle(c):
+            spread_done(stage, c, made)
+
+            @pl.when(more)
+            def _():
+                forward_z(c)
+
+            @pl.when(iteration == ITERS - 1)
+            def _():
+                out_ref[:, chunk(c)] = window[own_planes, chunk(c)]
+
+        pipeline(
+            [
+                lambda c: correct(iteration, c),
+                lambda c: reduce_pair(iteration, c),
+                lambda c: update(iteration, made, c),
+                lambda c: send_on(stage, c, made[1]),
+                lambda c: send_on(stage, c, made[2]),
+                settle,
+            ]
+        )
+        edges_sent(iteration)
+
+        def finish(c, carry_):
+            sums_sent(iteration, c)
+            return carry_
+
+        return lax.fori_loop(0, CHUNKS, finish, carry)
+
+    initial()
     cover_copy.wait_send()
     remote(cover.at[1 - side], cover.at[1 - side], cover_sem, 0, sibling).wait_recv()
     which = takes_lateral * views + view
     weight[:planes, :] = jnp.broadcast_to(cover[0, pl.ds(which, 1), :], (planes, columns))
     weight[planes:, :] = jnp.broadcast_to(cover[1, pl.ds(which, 1), :], (planes, columns))
-    for iteration in range(ITERS):
-        middle(iteration)
-        pipeline(
-            [
-                functools.partial(correct, iteration),
-                functools.partial(reduce_pair, iteration),
-                functools.partial(update, iteration),
-                functools.partial(spread_group, iteration + 1),
-                functools.partial(spread_beside, iteration + 1),
-                functools.partial(settle, iteration + 1),
-            ]
-        )
-        edges_sent(iteration)
-        for c in range(CHUNKS):
-            sums_sent(iteration, c)
+    lax.fori_loop(0, ITERS, one_pass, 0)
     views_sent()
 
 
@@ -802,7 +822,7 @@
             pltpu.VMEM((slab, lines, depth), F32),
             pltpu.VMEM((depth, slab, lines), F32),
             pltpu.VMEM((span, lines, columns), F32),
-            pltpu.VMEM((ITERS, 2 * span, lines, columns), F32),
+            pltpu.VMEM((ITERS * 2 * span, lines, columns), F32),
             pltpu.VMEM((span, lines, columns), F32),
             pltpu.VMEM((ITERS, 4, block, lines, columns), F32),
             pltpu.VMEM((ITERS, 3, block, lines, columns), F32),

time: 172 us -> 152 us (0.88)
  Pallas kernels: 165 us -> 145 us
    pallas_call x1, Pallas kernels: 165 us -> 145 us  [joint(): pl.pallas_call(functools.partial(joint_kernel, owners, views, planes, lin...]
where the time goes in v4:
time: 152 us
  Pallas kernels  145 us (95%)
  local copies, waits for them, and re-layouts  6.42 us (4%)
    pallas_call x1, Pallas kernels, joint(): pl.pallas_call(functools.partial(joint_kernel, owners, views, planes, lin...  145 us
    unnamed x13, local copies, waits for them, and re-layouts  5.95 us

profile of v4, /device:TPU:0, one launch (start us, length us, event | category | flops | bytes accessed | tf_op | source)
XLA Modules:
  0.0 151.6 jit_solution(8507992690728626593)
XLA Ops:
  0.0 0.0 copy-start.3
  0.0 0.7 copy-done.3
  0.7 0.0 copy-start.4
  0.7 0.0 copy-start.5
  0.7 0.1 copy.7
  0.8 0.6 copy-done.4
  1.4 0.0 copy-done.5
  1.4 0.1 fusion
  1.5 0.1 select_n.23
  1.6 0.1 div.11
  1.6 0.1 div.12
  1.7 0.1 broadcast_in_dim.4
  1.8 0.1 reshape.13.cover_ref
  1.9 0.0 copy-start
  1.9 1.2 copy-done
  3.1 0.0 copy-start.1
  3.1 1.2 copy-done.1
  4.4 0.0 copy-start.2
  4.4 1.2 copy-done.2
  5.6 145.0 %shard_map.64 = f32[16,128,128]{2,1,0:T(8,128)S(1)} custom-call(f32[99]{0:T(128)S(1)} %div.13.psf_ref, f32[16,128,128]{2,1,0:T(8,128)S(1)} %copy-done, f32[16,128,128]{2,1,0:T(8,128)S(1)} %bitcast.6, f32[16,128,128]{2,1,0:T(8,128)S(1)} %bitcast.7, f32[8,128]{1,0:T(8,128)S(1)} %reshape.13.cover_ref), custom_call_target="tpu_custom_call" | custom-call | tf_op jit(solution)/shard_map/pallas_call | solution.py:814
  150.6 1.0 copy.9
  (2 shorter events, 0.0 us)
Async XLA Ops:
  0.0 0.7 copy-start.3
  0.7 0.7 copy-start.4
  0.7 0.7 copy-start.5
  1.9 1.2 copy-start
  3.1 1.2 copy-start.1
  4.4 1.2 copy-start.2

commit v5 on v4

--- a/solution.py
+++ b/solution.py
@@ -171,6 +171,8 @@
 MESH = pl.DeviceIdType.MESH
 CHUNKS = 4
 PARTS = 2
+EDGE = 4
+GROUP = 8
 
 
 def split_bf16(values):
@@ -555,38 +557,39 @@
         result = dot32(matrix[...], jnp.concatenate([high, low], axis=0))
         return result[:lines] + result[lines:]
 
-    def side_by_side(stacked):
-        return jnp.concatenate([stacked[:lines], stacked[lines:]], axis=1)
-
-    def stacked_up(beside):
-        return jnp.concatenate([beside[:, :columns], beside[:, columns:]], axis=0)
-
     window_lines = window.reshape(2 * span * lines, columns)
     mid_lines = mid.reshape(span * lines, columns)
     logs_lines = logs.reshape(span * lines, columns)
     quot_lines = quot.reshape(ITERS * 2 * span * lines, columns)
 
+    def z_then_x(source, z_matrix, x_matrix, y, first_row=0):
+        results = []
+        for step in range(0, GROUP, 2):
+            results.extend(along_z(source, z_matrix, y + step, first_row))
+        return along_x(jnp.concatenate(results, axis=0), x_matrix)
+
     def forward_z(c):
         def lines_of(i, carry):
-            for step in range(4):
-                y = c * chunk_lines + i * 8 + 2 * step
-                one, two = along_z(window_lines, z_fwd, y)
-                mid_lines[pl.ds(y, span, stride=lines), :] = one
-                mid_lines[pl.ds(y + 1, span, stride=lines), :] = two
+            y = c * chunk_lines + i * GROUP
+            result = z_then_x(window_lines, z_fwd, x_fwd, y)
+            for step in range(GROUP):
+                mid_lines[pl.ds(y + step, span, stride=lines), :] = result[
+                    step * span : (step + 1) * span
+                ]
             return carry
 
-        lax.fori_loop(0, chunk_lines // 8, lines_of, 0)
+        lax.fori_loop(0, chunk_lines // GROUP, lines_of, 0)
 
     def plane_pair(iteration, z):
-        blurred = along_x(mid[pl.ds(z, 2)].reshape(2 * lines, columns), x_fwd)
-        blurred = along_y(side_by_side(blurred), y_fwd)
+        blurred = along_y(jnp.concatenate([mid[z], mid[z + 1]], axis=1), y_fwd)
         seen = jnp.concatenate([observed[z], observed[z + 1]], axis=1)
         back = along_y(seen / blurred, y_back)
-        back = along_x(stacked_up(back), x_back)
-        quot[pl.ds(iteration * 2 * span + planes + z, 2)] = back.reshape(2, lines, columns)
+        first = iteration * 2 * span + planes + z
+        quot[first] = back[:, :columns]
+        quot[first + 1] = back[:, columns:]
 
     early = CHUNKS // 2
-    steps = planes // 2
+    steps = planes // EDGE
 
     def edge(iteration, index, up, plane, count, lines_at):
         start_plane = (2 * planes if up else planes) + plane
@@ -602,15 +605,16 @@
         )
 
     def early_edge(iteration, s, up):
-        return edge(iteration, s, up, 2 * s, 2, pl.ds(0, early * chunk_lines))
+        return edge(iteration, s, up, EDGE * s, EDGE, pl.ds(0, early * chunk_lines))
 
     def late_edge(iteration, c, up):
         return edge(iteration, steps + c - early, up, 0, planes, chunk(c))
 
     def middle(iteration):
         def step(s, carry):
-            plane_pair(iteration, 2 * s)
-            plane_pair(iteration, planes + 2 * s)
+            for k in range(0, EDGE, 2):
+                plane_pair(iteration, EDGE * s + k)
+                plane_pair(iteration, planes + EDGE * s + k)
             pl.when(has_below)(early_edge(iteration, s, False).start)
             pl.when(has_above)(early_edge(iteration, s, True).start)
             return carry
@@ -652,14 +656,15 @@
         first_row = iteration * 2 * span * lines
 
         def lines_of(i, carry):
-            for part_ in range(4):
-                y = c * chunk_lines + i * 8 + 2 * part_
-                for step, back in enumerate(along_z(quot_lines, z_back, y, first_row)):
-                    value = jnp.log(back) - (log_z[...] + log_xy[pl.ds(y + step, 1), :])
-                    logs_lines[pl.ds(y + step, span, stride=lines), :] = weight[...] * value
+            y = c * chunk_lines + i * GROUP
+            back = jnp.log(z_then_x(quot_lines, z_back, x_back, y, first_row))
+            for step in range(GROUP):
+                value = back[step * span : (step + 1) * span]
+                value = value - (log_z[...] + log_xy[pl.ds(y + step, 1), :])
+                logs_lines[pl.ds(y + step, span, stride=lines), :] = weight[...] * value
             return carry
 
-        lax.fori_loop(0, chunk_lines // 8, lines_of, 0)
+        lax.fori_loop(0, chunk_lines // GROUP, lines_of, 0)
 
     kinds = [(1, 1), (1, 0), (0, 1), (0, 0)]
 
@@ -839,7 +844,7 @@
             dma((2, 1)),
             dma((2, PARTS)),
             dma((2, owners, PARTS, 2)),
-            dma((2, ITERS, 2, planes // 2 + CHUNKS)),
+            dma((2, ITERS, 2, planes // EDGE + CHUNKS)),
             dma((2, ITERS + 1, CHUNKS, 4 * views)),
             dma((2, ITERS, CHUNKS, 4)),
             dma((2, ITERS, CHUNKS, 4)),
@@ -873,10 +878,10 @@
         and views == 4
         and owners % 2 == 0
         and planes % views == 0
-        and planes % (2 * PARTS) == 0
+        and planes % (EDGE * PARTS) == 0
         and rim <= planes
         and columns // owners % 8 == 0
-        and lines % (8 * CHUNKS) == 0
+        and lines % (GROUP * CHUNKS) == 0
     )
     body = joint if fits else local
     return body(estimate, axial_views, lateral_views, psf_axial, psf_lateral, coverage)

time: 152 us -> 154 us (1.013)
  Pallas kernels: 145 us -> 147 us
    pallas_call x1, Pallas kernels: 145 us -> 147 us  [joint(): pl.pallas_call(functools.partial(joint_kernel, owners, views, planes, lin...]
where the time goes in v5:
time: 154 us
  Pallas kernels  147 us (95%)
  local copies, waits for them, and re-layouts  6.42 us (4%)
    pallas_call x1, Pallas kernels, joint(): pl.pallas_call(functools.partial(joint_kernel, owners, views, planes, lin...  147 us
    unnamed x13, local copies, waits for them, and re-layouts  5.95 us

profile of v5, /device:TPU:0, one launch (start us, length us, event | category | flops | bytes accessed | tf_op | source)
XLA Modules:
  0.0 153.8 jit_solution(5418960576020411472)
XLA Ops:
  0.0 0.0 copy-start.3
  0.0 0.7 copy-done.3
  0.7 0.0 copy-start.4
  0.7 0.0 copy-start.5
  0.7 0.1 copy.7
  0.8 0.6 copy-done.4
  1.4 0.0 copy-done.5
  1.4 0.1 fusion
  1.5 0.1 select_n.23
  1.6 0.1 div.11
  1.6 0.1 div.12
  1.7 0.1 broadcast_in_dim.4
  1.8 0.1 reshape.13.cover_ref
  1.9 0.0 copy-start
  1.9 1.2 copy-done
  3.1 0.0 copy-start.1
  3.1 1.2 copy-done.1
  4.4 0.0 copy-start.2
  4.4 1.2 copy-done.2
  5.6 147.3 %shard_map.64 = f32[16,128,128]{2,1,0:T(8,128)S(1)} custom-call(f32[99]{0:T(128)S(1)} %div.13.psf_ref, f32[16,128,128]{2,1,0:T(8,128)S(1)} %copy-done, f32[16,128,128]{2,1,0:T(8,128)S(1)} %bitcast.6, f32[16,128,128]{2,1,0:T(8,128)S(1)} %bitcast.7, f32[8,128]{1,0:T(8,128)S(1)} %reshape.13.cover_ref), custom_call_target="tpu_custom_call" | custom-call | tf_op jit(solution)/shard_map/pallas_call | solution.py:819
  152.9 1.0 copy.9
  (2 shorter events, 0.0 us)
Async XLA Ops:
  0.0 0.7 copy-start.3
  0.7 0.7 copy-start.4
  0.7 0.7 copy-start.5
  1.9 1.2 copy-start
  3.1 1.2 copy-start.1
  4.4 1.2 copy-start.2

commit v6 on v5

--- a/solution.py
+++ b/solution.py
@@ -261,25 +261,26 @@
                 device_id=device(side_, lax.rem(view + step, views)),
                 device_id_type=MESH,
             )
-    own_planes = pl.ds(planes + planes * side, planes)
-    estimate_in = pltpu.make_async_copy(estimate_ref, window.at[own_planes], local_sem.at[0])
+    mine = window.at[pl.ds(2 + 2 * side, 2)]
+    estimate_in = pltpu.make_async_copy(estimate_ref, mine, local_sem.at[0])
     lateral_in = pltpu.make_async_copy(lateral_ref, lateral, local_sem.at[1])
+    window_planes = window.reshape(2 * span, lines, columns)
     estimate_in.start()
     lateral_in.start()
     cover[pl.ds(side, 1)] = cover_ref[...][None]
 
-    def clear(base):
+    def clear(slab_):
         def plane(z, carry):
             zero = jnp.zeros((lines, columns), F32)
-            window[base + z] = zero
+            window_planes[slab_ * planes + z] = zero
             for iteration in range(ITERS):
-                quot[iteration * 2 * span + base + z] = zero
+                quot[iteration * 2 * span + slab_ * planes + z] = zero
             return carry
 
         lax.fori_loop(0, planes, plane, 0)
 
     pl.when(group == 0)(lambda: clear(0))
-    pl.when(group == groups - 1)(lambda: clear(3 * planes))
+    pl.when(group == groups - 1)(lambda: clear(3))
 
     estimate_in.wait()
     pl.semaphore_wait(barrier, owners - 1 + 2 * (views - 1))
@@ -297,90 +298,106 @@
     def chunk(c):
         return pl.ds(pl.multiple_of(c * chunk_lines, chunk_lines), chunk_lines)
 
-    def part(e, c):
-        return window.at[pl.ds(e * block, block), chunk(c)]
-
-    def slot_of(side_, row_, core_):
-        return views + views * side_ + 2 * row_ + core_
-
-    def copy_part(stage, c, e_src, e_dst, slot, target):
+    def part(first, count, core_, c):
+        return window.at[pl.ds(first, count), core_, :, chunk(c)]
+
+    def copy_part(stage, c, slot, src, dst, count, target):
         return pltpu.make_async_remote_copy(
-            src_ref=part(e_src, c),
-            dst_ref=part(e_dst, c),
+            src_ref=part(src, count, core, c),
+            dst_ref=part(dst, count, core, c),
             send_sem=share_sem.at[0, stage, c, slot],
-            recv_sem=share_sem.at[1, stage, c, e_dst],
+            recv_sem=share_sem.at[1, stage, c, slot],
             device_id=target,
             device_id_type=MESH,
         )
 
-    def arrival(stage, c, e):
-        return copy_part(stage, c, e, e, 0, sibling)
-
-    own = slot_of(side, row, core)
+    own = 2 + 2 * side + row
+    own_side = 2 + 2 * side
+    other_side = 4 - 2 * side
     row_peer = device(side, 2 * (1 - row) + core)
     side_peer = device(1 - side, view)
     far_peer = device(1 - side, 2 * (1 - row) + core)
     other = 1 - core
     yes = group >= 0
 
-    def block_of(kind):
-        side_ = lax.rem(side + kind[0], 2)
-        row_ = lax.rem(row + kind[1], 2)
-        return side_, slot_of(side_, row_, core)
-
-    def beside(more, kind):
-        side_, e = block_of(kind)
-        to = group + 2 * side_ - 1
-        valid = (to >= 0) & (to < groups) & more
-        e_dst = e + (1 - 3 * side_) * views + (1 - side_) * views
-        return valid, e, e_dst, 4 + 2 * kind[0] + kind[1], (2 * to + side, view)
+    def up_copy(more):
+        return (has_above & more, 3, 4, 0, 2, (me + 2, view))
+
+    def down_copy(more):
+        return (has_below & more, 4, 2, 6, 2, (me - 2, view))
 
     def plan(first, more):
+        x_arrival = (more, 0, 2 + 2 * (1 - side) + row, 1, core)
+        y_arrival = (yes, 1, 2 + 2 * side + 1 - row, 1, core)
+        far_arrival = (more, 2, 2 + 2 * (1 - side) + 1 - row, 1, core)
         if first:
-            at_once = [(yes, own, own, 0, side_peer), beside(yes, (0, 0)), beside(yes, (0, 1))]
+            near = (has_above & (side == 1), 3, 4, 0, 2, (me + 2, view))
+            near_down = (has_below & (side == 0), 4, 2, 6, 2, (me - 2, view))
+            at_once = [(yes, 0, own, own, 1, side_peer), near, near_down]
+            across = x_arrival[2]
+            group_steps = [
+                ([x_arrival], [(yes, 2, across, across, 1, row_peer)]),
+                (
+                    [far_arrival],
+                    [
+                        (yes, 5, other_side, other_side, 2, sibling),
+                        (has_above & (side == 0), 3, 4, 0, 2, (me + 2, view)),
+                        (has_below & (side == 1), 4, 2, 6, 2, (me - 2, view)),
+                    ],
+                ),
+            ]
+            rest = [(yes, 5, other_side, 2, other)]
         else:
             at_once = [
-                (more, own, own, 0, side_peer),
-                (yes, own, own, 1, row_peer),
-                (yes, own, own, 2, sibling),
-                (more, own, own, 3, far_peer),
-                beside(more, (0, 0)),
+                (more, 0, own, own, 1, side_peer),
+                (yes, 1, own, own, 1, row_peer),
+                (more, 2, own, own, 1, far_peer),
             ]
-        group_steps = []
-        for kind in [(1, 0), (1, 1)] if first else [(0, 1), (1, 0), (1, 1)]:
-            e = block_of(kind)[1]
-            when = yes if kind == (0, 1) else more
-            onward = [beside(more, kind), (when, e, e, 8 + 2 * kind[0] + kind[1], sibling)]
-            if first and kind == (1, 0):
-                onward.append((yes, e, e, 3, row_peer))
-            group_steps.append((when, e, onward))
-        beside_steps = []
-        rest = []
-        for row_ in (0, 1):
-            for k, base, condition in ((0, 0, has_below), (1, 3 * views, has_above)):
-                e = base + 2 * row_ + core
-                onward = [(condition & more, e, e, 12 + 2 * row_ + k, sibling)]
-                beside_steps.append((condition & more, e, onward))
-                rest.append((condition & more, base + 2 * row_ + other))
-            if not first:
-                rest.append((yes, slot_of(side, row_, other)))
-            rest.append((more, slot_of(1 - side, row_, other)))
+            group_steps = [
+                (
+                    [y_arrival, x_arrival, far_arrival],
+                    [
+                        up_copy(more),
+                        down_copy(more),
+                        (more, 5, 2, 2, 4, sibling),
+                        (jnp.logical_not(more), 8, own_side, own_side, 2, sibling),
+                    ],
+                )
+            ]
+            rest = [(more, 5, 2, 4, other), (jnp.logical_not(more), 8, own_side, 2, other)]
+        beside_steps = [
+            ([(has_below & more, 3, 0, 2, core)], [(has_below & more, 6, 0, 0, 2, sibling)]),
+            ([(has_above & more, 4, 6, 2, core)], [(has_above & more, 7, 6, 6, 2, sibling)]),
+        ]
+        rest = rest + [(has_below & more, 6, 0, 2, other), (has_above & more, 7, 6, 2, other)]
         return at_once, group_steps, beside_steps, rest
 
     def start_all(stage, c, sends):
         for condition, *where in sends:
             pl.when(condition)(copy_part(stage, c, *where).start)
 
+    def await_all(stage, c, arrivals):
+        for condition, slot, first, count, core_ in arrivals:
+            there = part(first, count, core_, c)
+            made = pltpu.make_async_remote_copy(
+                src_ref=there,
+                dst_ref=there,
+                send_sem=share_sem.at[0, stage, c, slot],
+                recv_sem=share_sem.at[1, stage, c, slot],
+                device_id=sibling,
+                device_id_type=MESH,
+            )
+            pl.when(condition)(made.wait_recv)
+
     def send_on(stage, c, steps_):
-        for condition, e, onward in steps_:
-            pl.when(condition)(arrival(stage, c, e).wait_recv)
+        for arrivals, onward in steps_:
+            await_all(stage, c, arrivals)
             start_all(stage, c, onward)
 
     def spread_done(stage, c, made):
         at_once, group_steps, beside_steps, rest = made
-        for condition, e in rest:
-            pl.when(condition)(arrival(stage, c, e).wait_recv)
-        onwards = [onward for _, _, onward in group_steps + beside_steps]
+        await_all(stage, c, rest)
+        onwards = [onward for _, onward in group_steps + beside_steps]
         for condition, *where in sum(onwards, at_once):
             pl.when(condition)(copy_part(stage, c, *where).wait_send)
 
@@ -666,19 +683,14 @@
 
         lax.fori_loop(0, chunk_lines // GROUP, lines_of, 0)
 
-    kinds = [(1, 1), (1, 0), (0, 1), (0, 0)]
-
-    def log_block(kind, core_):
-        side_ = lax.rem(side + kind[0], 2)
-        row_ = lax.rem(row + kind[1], 2)
-        return pl.ds((views * side_ + 2 * row_ + core_) * block, block)
-
-    def to_sibling(iteration, c, k):
+    kinds = [(1, 1), (1, 0), (0, 1)]
+
+    def to_sibling(iteration, c):
         return pltpu.make_async_remote_copy(
-            src_ref=logs.at[log_block(kinds[k], 1 - core), chunk(c)],
-            dst_ref=pair_sum.at[iteration, k, :, chunk(c)],
-            send_sem=pair_sem.at[0, iteration, c, k],
-            recv_sem=pair_sem.at[1, iteration, c, k],
+            src_ref=logs.at[:, other, :, chunk(c)],
+            dst_ref=pair_sum.at[iteration, :, :, chunk(c)],
+            send_sem=pair_sem.at[0, iteration, c],
+            recv_sem=pair_sem.at[1, iteration, c],
             device_id=sibling,
             device_id_type=MESH,
         )
@@ -687,7 +699,7 @@
         side_ = lax.rem(side + kinds[k][0], 2)
         row_ = lax.rem(row + kinds[k][1], 2)
         return pltpu.make_async_remote_copy(
-            src_ref=logs.at[log_block(kinds[k], core), chunk(c)],
+            src_ref=logs.at[2 * side_ + row_, core, :, chunk(c)],
             dst_ref=peer_sum.at[iteration, k, :, chunk(c)],
             send_sem=peer_sem.at[0, iteration, c, k],
             recv_sem=peer_sem.at[1, iteration, c, k],
@@ -698,31 +710,30 @@
     def correct(iteration, c):
         edges_arrived(iteration, c)
         backward_z(iteration, c)
+        to_sibling(iteration, c).start()
+
+    def reduce_pair(iteration, c):
+        to_sibling(iteration, c).wait_recv()
         for k in range(4):
-            to_sibling(iteration, c, k).start()
-
-    def reduce_pair(iteration, c):
-        for k in range(4):
-            to_sibling(iteration, c, k).wait_recv()
-            mine = log_block(kinds[k], core)
-            logs[mine, chunk(c)] = logs[mine, chunk(c)] + pair_sum[iteration, k, :, chunk(c)]
-            if k < 3:
-                to_peer(iteration, c, k).start()
+            logs[k, core, :, chunk(c)] = (
+                logs[k, core, :, chunk(c)] + pair_sum[iteration, k, :, chunk(c)]
+            )
+        for k in range(3):
+            to_peer(iteration, c, k).start()
 
     def update(iteration, made, c):
         for k in (1, 2, 0):
             to_peer(iteration, c, k).wait_recv()
         count = jnp.sum(cover_ref[...], axis=0, keepdims=True)
-        total = logs[log_block((0, 0), core), chunk(c)]
+        total = logs[2 * side + row, core, :, chunk(c)]
         for k in range(3):
             total = total + peer_sum[iteration, k, :, chunk(c)]
-        here = pl.ds(own * block, block)
-        window[here, chunk(c)] = window[here, chunk(c)] * jnp.exp(total / count[None])
+        factor = jnp.exp(total / count[None])
+        window[own, core, :, chunk(c)] = window[own, core, :, chunk(c)] * factor
         start_all(iteration + 1, c, made[0])
 
     def sums_sent(iteration, c):
-        for k in range(4):
-            to_sibling(iteration, c, k).wait_send()
+        to_sibling(iteration, c).wait_send()
         for k in range(3):
             to_peer(iteration, c, k).wait_send()
 
@@ -771,7 +782,7 @@
 
             @pl.when(iteration == ITERS - 1)
             def _():
-                out_ref[:, chunk(c)] = window[own_planes, chunk(c)]
+                out_ref[:, :, :, chunk(c)] = window[pl.ds(own_side, 2), :, :, chunk(c)]
 
         pipeline(
             [
@@ -818,17 +829,17 @@
     dma = pltpu.SemaphoreType.DMA
     result = pl.pallas_call(
         functools.partial(joint_kernel, owners, views, planes, lines, columns),
-        out_shape=jax.ShapeDtypeStruct((planes, lines, columns), F32),
+        out_shape=jax.ShapeDtypeStruct((2, 2, block, lines, columns), F32),
         in_specs=[pl.BlockSpec(memory_space=pltpu.SMEM)] + [hbm] * 3 + [vmem],
         out_specs=vmem,
         scratch_shapes=[
-            pltpu.VMEM((2 * span, lines, columns), F32),
+            pltpu.VMEM((8, 2, block, lines, columns), F32),
             pltpu.VMEM((span, lines, columns), F32),
             pltpu.VMEM((slab, lines, depth), F32),
             pltpu.VMEM((depth, slab, lines), F32),
             pltpu.VMEM((span, lines, columns), F32),
             pltpu.VMEM((ITERS * 2 * span, lines, columns), F32),
-            pltpu.VMEM((span, lines, columns), F32),
+            pltpu.VMEM((4, 2, block, lines, columns), F32),
             pltpu.VMEM((ITERS, 4, block, lines, columns), F32),
             pltpu.VMEM((ITERS, 3, block, lines, columns), F32),
             pltpu.VMEM((2,) + cover.shape, F32),
@@ -845,9 +856,9 @@
             dma((2, PARTS)),
             dma((2, owners, PARTS, 2)),
             dma((2, ITERS, 2, planes // EDGE + CHUNKS)),
-            dma((2, ITERS + 1, CHUNKS, 4 * views)),
-            dma((2, ITERS, CHUNKS, 4)),
-            dma((2, ITERS, CHUNKS, 4)),
+            dma((2, ITERS + 1, CHUNKS, 9)),
+            dma((2, ITERS, CHUNKS)),
+            dma((2, ITERS, CHUNKS, 3)),
             dma((3,)),
         ],
         compiler_params=pltpu.CompilerParams(
@@ -855,12 +866,12 @@
         ),
     )(
         psf.reshape(-1),
-        estimate,
+        estimate.reshape(2, 2, block, lines, columns),
         axial_views[0],
         lateral_views[0],
         cover,
     )
-    return result
+    return result.reshape(planes, lines, columns)
 
 
 def chosen(estimate, axial_views, lateral_views, psf_axial, psf_lateral, coverage):

time: 154 us -> 153 us (level)
  no operation moved by 1% of the time
where the time goes in v6:
time: 153 us
  Pallas kernels  146 us (95%)
  local copies, waits for them, and re-layouts  6.42 us (4%)
    pallas_call x1, Pallas kernels, joint(): pl.pallas_call(functools.partial(joint_kernel, owners, views, planes, lin...  146 us
    unnamed x13, local copies, waits for them, and re-layouts  5.95 us

profile of v6, /device:TPU:0, one launch (start us, length us, event | category | flops | bytes accessed | tf_op | source)
XLA Modules:
  0.0 153.1 jit_solution(13073245087279125551)
XLA Ops:
  0.0 0.0 copy-start.3
  0.0 0.7 copy-done.3
  0.7 0.0 copy-start.4
  0.7 0.0 copy-start.5
  0.7 0.1 copy.7
  0.8 0.6 copy-done.4
  1.4 0.0 copy-done.5
  1.4 0.1 fusion
  1.5 0.1 select_n.23
  1.6 0.1 div.11
  1.6 0.1 div.12
  1.7 0.1 broadcast_in_dim.4
  1.8 0.1 reshape.20.cover_ref
  1.9 0.0 copy-start
  1.9 1.2 copy-done
  3.1 0.0 copy-start.1
  3.1 1.2 copy-done.1
  4.4 0.0 copy-start.2
  4.4 1.2 copy-done.2
  5.6 146.5 %shard_map.64 = f32[2,2,4,128,128]{4,3,2,1,0:T(8,128)S(1)} custom-call(f32[99]{0:T(128)S(1)} %div.13.psf_ref, f32[2,2,4,128,128]{4,3,2,1,0:T(8,128)S(1)} %bitcast.9, f32[16,128,128]{2,1,0:T(8,128)S(1)} %bitcast.10, f32[16,128,128]{2,1,0:T(8,128)S(1)} %bitcast.11, f32[8,128]{1,0:T(8,128)S(1)} %reshape.20.cover_ref), custom_call_target="tpu_custom_call" | custom-call | tf_op jit(solution)/shard_map/pallas_call | solution.py:830
  152.1 1.0 copy.9
  (2 shorter events, 0.0 us)
Async XLA Ops:
  0.0 0.7 copy-start.3
  0.7 0.7 copy-start.4
  0.7 0.7 copy-start.5
  1.9 1.2 copy-start
  3.1 1.2 copy-start.1
  4.4 1.2 copy-start.2

commit v7 on v6

--- a/solution.py
+++ b/solution.py
@@ -169,7 +169,7 @@
 F32 = jnp.float32
 BF16 = jnp.bfloat16
 MESH = pl.DeviceIdType.MESH
-CHUNKS = 4
+CHUNKS = 2
 PARTS = 2
 EDGE = 4
 GROUP = 8
@@ -331,20 +331,29 @@
         y_arrival = (yes, 1, 2 + 2 * side + 1 - row, 1, core)
         far_arrival = (more, 2, 2 + 2 * (1 - side) + 1 - row, 1, core)
         if first:
-            near = (has_above & (side == 1), 3, 4, 0, 2, (me + 2, view))
-            near_down = (has_below & (side == 0), 4, 2, 6, 2, (me - 2, view))
+            near = (has_above & (side == 1), 3, 4 + row, row, 1, (me + 2, view))
+            near_down = (has_below & (side == 0), 4, 2 + row, 6 + row, 1, (me - 2, view))
             at_once = [(yes, 0, own, own, 1, side_peer), near, near_down]
             across = x_arrival[2]
             group_steps = [
-                ([x_arrival], [(yes, 2, across, across, 1, row_peer)]),
                 (
-                    [far_arrival],
+                    [x_arrival],
                     [
-                        (yes, 5, other_side, other_side, 2, sibling),
-                        (has_above & (side == 0), 3, 4, 0, 2, (me + 2, view)),
-                        (has_below & (side == 1), 4, 2, 6, 2, (me - 2, view)),
+                        (yes, 2, across, across, 1, row_peer),
+                        (has_above & (side == 0), 3, 4 + row, row, 1, (me + 2, view)),
+                        (has_below & (side == 1), 4, 2 + row, 6 + row, 1, (me - 2, view)),
                     ],
                 ),
+                ([far_arrival], [(yes, 5, other_side, other_side, 2, sibling)]),
+            ]
+            beside_steps = [
+                ([(has_below, 3, row, 1, core)], [(has_below, 9, row, row, 1, row_peer)]),
+                (
+                    [(has_above, 4, 6 + row, 1, core)],
+                    [(has_above, 10, 6 + row, 6 + row, 1, row_peer)],
+                ),
+                ([(has_below, 9, 1 - row, 1, core)], [(has_below, 6, 0, 0, 2, sibling)]),
+                ([(has_above, 10, 7 - row, 1, core)], [(has_above, 7, 6, 6, 2, sibling)]),
             ]
             rest = [(yes, 5, other_side, 2, other)]
         else:
@@ -364,11 +373,11 @@
                     ],
                 )
             ]
+            beside_steps = [
+                ([(has_below & more, 3, 0, 2, core)], [(has_below & more, 6, 0, 0, 2, sibling)]),
+                ([(has_above & more, 4, 6, 2, core)], [(has_above & more, 7, 6, 6, 2, sibling)]),
+            ]
             rest = [(more, 5, 2, 4, other), (jnp.logical_not(more), 8, own_side, 2, other)]
-        beside_steps = [
-            ([(has_below & more, 3, 0, 2, core)], [(has_below & more, 6, 0, 0, 2, sibling)]),
-            ([(has_above & more, 4, 6, 2, core)], [(has_above & more, 7, 6, 6, 2, sibling)]),
-        ]
         rest = rest + [(has_below & more, 6, 0, 2, other), (has_above & more, 7, 6, 2, other)]
         return at_once, group_steps, beside_steps, rest
 
@@ -856,7 +865,7 @@
             dma((2, PARTS)),
             dma((2, owners, PARTS, 2)),
             dma((2, ITERS, 2, planes // EDGE + CHUNKS)),
-            dma((2, ITERS + 1, CHUNKS, 9)),
+            dma((2, ITERS + 1, CHUNKS, 11)),
             dma((2, ITERS, CHUNKS)),
             dma((2, ITERS, CHUNKS, 3)),
             dma((3,)),

time: 153 us -> 172 us (1.12)
  Pallas kernels: 146 us -> 165 us
    pallas_call x1, Pallas kernels: 146 us -> 165 us  [joint(): pl.pallas_call(functools.partial(joint_kernel, owners, views, planes, lin...]
where the time goes in v7:
time: 172 us
  Pallas kernels  165 us (96%)
  local copies, waits for them, and re-layouts  6.42 us (4%)
    pallas_call x1, Pallas kernels, joint(): pl.pallas_call(functools.partial(joint_kernel, owners, views, planes, lin...  165 us
    unnamed x13, local copies, waits for them, and re-layouts  5.95 us

profile of v7, /device:TPU:0, one launch (start us, length us, event | category | flops | bytes accessed | tf_op | source)
XLA Modules:
  0.0 171.5 jit_solution(13131845291073751780)
XLA Ops:
  0.0 0.0 copy-start.3
  0.0 0.7 copy-done.3
  0.7 0.0 copy-start.4
  0.7 0.0 copy-start.5
  0.7 0.1 copy.7
  0.8 0.6 copy-done.4
  1.4 0.0 copy-done.5
  1.4 0.1 fusion
  1.5 0.1 select_n.23
  1.6 0.1 div.11
  1.6 0.1 div.12
  1.7 0.1 broadcast_in_dim.4
  1.8 0.1 reshape.20.cover_ref
  1.9 0.0 copy-start
  1.9 1.2 copy-done
  3.1 0.0 copy-start.1
  3.1 1.2 copy-done.1
  4.4 0.0 copy-start.2
  4.4 1.2 copy-done.2
  5.6 165.0 %shard_map.64 = f32[2,2,4,128,128]{4,3,2,1,0:T(8,128)S(1)} custom-call(f32[99]{0:T(128)S(1)} %div.13.psf_ref, f32[2,2,4,128,128]{4,3,2,1,0:T(8,128)S(1)} %bitcast.9, f32[16,128,128]{2,1,0:T(8,128)S(1)} %bitcast.10, f32[16,128,128]{2,1,0:T(8,128)S(1)} %bitcast.11, f32[8,128]{1,0:T(8,128)S(1)} %reshape.20.cover_ref), custom_call_target="tpu_custom_call" | custom-call | tf_op jit(solution)/shard_map/pallas_call | solution.py:839
  170.6 1.0 copy.9
  (2 shorter events, 0.0 us)
Async XLA Ops:
  0.0 0.7 copy-start.3
  0.7 0.7 copy-start.4
  0.7 0.7 copy-start.5
  1.9 1.2 copy-start
  3.1 1.2 copy-start.1
  4.4 1.2 copy-start.2

commit v8 on v6

--- a/solution.py
+++ b/solution.py
@@ -171,8 +171,6 @@
 MESH = pl.DeviceIdType.MESH
 CHUNKS = 4
 PARTS = 2
-EDGE = 4
-GROUP = 8
 
 
 def split_bf16(values):
@@ -574,39 +572,38 @@
         result = dot32(matrix[...], jnp.concatenate([high, low], axis=0))
         return result[:lines] + result[lines:]
 
+    def side_by_side(stacked):
+        return jnp.concatenate([stacked[:lines], stacked[lines:]], axis=1)
+
+    def stacked_up(beside):
+        return jnp.concatenate([beside[:, :columns], beside[:, columns:]], axis=0)
+
     window_lines = window.reshape(2 * span * lines, columns)
     mid_lines = mid.reshape(span * lines, columns)
     logs_lines = logs.reshape(span * lines, columns)
     quot_lines = quot.reshape(ITERS * 2 * span * lines, columns)
 
-    def z_then_x(source, z_matrix, x_matrix, y, first_row=0):
-        results = []
-        for step in range(0, GROUP, 2):
-            results.extend(along_z(source, z_matrix, y + step, first_row))
-        return along_x(jnp.concatenate(results, axis=0), x_matrix)
-
     def forward_z(c):
         def lines_of(i, carry):
-            y = c * chunk_lines + i * GROUP
-            result = z_then_x(window_lines, z_fwd, x_fwd, y)
-            for step in range(GROUP):
-                mid_lines[pl.ds(y + step, span, stride=lines), :] = result[
-                    step * span : (step + 1) * span
-                ]
+            for step in range(4):
+                y = c * chunk_lines + i * 8 + 2 * step
+                one, two = along_z(window_lines, z_fwd, y)
+                mid_lines[pl.ds(y, span, stride=lines), :] = one
+                mid_lines[pl.ds(y + 1, span, stride=lines), :] = two
             return carry
 
-        lax.fori_loop(0, chunk_lines // GROUP, lines_of, 0)
+        lax.fori_loop(0, chunk_lines // 8, lines_of, 0)
 
     def plane_pair(iteration, z):
-        blurred = along_y(jnp.concatenate([mid[z], mid[z + 1]], axis=1), y_fwd)
+        blurred = along_x(mid[pl.ds(z, 2)].reshape(2 * lines, columns), x_fwd)
+        blurred = along_y(side_by_side(blurred), y_fwd)
         seen = jnp.concatenate([observed[z], observed[z + 1]], axis=1)
         back = along_y(seen / blurred, y_back)
-        first = iteration * 2 * span + planes + z
-        quot[first] = back[:, :columns]
-        quot[first + 1] = back[:, columns:]
+        back = along_x(stacked_up(back), x_back)
+        quot[pl.ds(iteration * 2 * span + planes + z, 2)] = back.reshape(2, lines, columns)
 
     early = CHUNKS // 2
-    steps = planes // EDGE
+    steps = planes // 2
 
     def edge(iteration, index, up, plane, count, lines_at):
         start_plane = (2 * planes if up else planes) + plane
@@ -622,16 +619,15 @@
         )
 
     def early_edge(iteration, s, up):
-        return edge(iteration, s, up, EDGE * s, EDGE, pl.ds(0, early * chunk_lines))
+        return edge(iteration, s, up, 2 * s, 2, pl.ds(0, early * chunk_lines))
 
     def late_edge(iteration, c, up):
         return edge(iteration, steps + c - early, up, 0, planes, chunk(c))
 
     def middle(iteration):
         def step(s, carry):
-            for k in range(0, EDGE, 2):
-                plane_pair(iteration, EDGE * s + k)
-                plane_pair(iteration, planes + EDGE * s + k)
+            plane_pair(iteration, 2 * s)
+            plane_pair(iteration, planes + 2 * s)
             pl.when(has_below)(early_edge(iteration, s, False).start)
             pl.when(has_above)(early_edge(iteration, s, True).start)
             return carry
@@ -673,15 +669,14 @@
         first_row = iteration * 2 * span * lines
 
         def lines_of(i, carry):
-            y = c * chunk_lines + i * GROUP
-            back = jnp.log(z_then_x(quot_lines, z_back, x_back, y, first_row))
-            for step in range(GROUP):
-                value = back[step * span : (step + 1) * span]
-                value = value - (log_z[...] + log_xy[pl.ds(y + step, 1), :])
-                logs_lines[pl.ds(y + step, span, stride=lines), :] = weight[...] * value
+            for part_ in range(4):
+                y = c * chunk_lines + i * 8 + 2 * part_
+                for step, back in enumerate(along_z(quot_lines, z_back, y, first_row)):
+                    value = jnp.log(back) - (log_z[...] + log_xy[pl.ds(y + step, 1), :])
+                    logs_lines[pl.ds(y + step, span, stride=lines), :] = weight[...] * value
             return carry
 
-        lax.fori_loop(0, chunk_lines // GROUP, lines_of, 0)
+        lax.fori_loop(0, chunk_lines // 8, lines_of, 0)
 
     kinds = [(1, 1), (1, 0), (0, 1)]
 
@@ -757,15 +752,19 @@
         start_axial()
         turn()
         start_lateral()
+
+        def forward_group(c, carry):
+            send_on(0, c, made[1])
+            return carry
+
+        lax.fori_loop(0, CHUNKS, forward_group, 0)
         prepare()
 
         def settle(c):
             spread_done(0, c, made)
             forward_z(c)
 
-        pipeline(
-            [lambda c: send_on(0, c, made[1]), lambda c: send_on(0, c, made[2]), settle]
-        )
+        pipeline([lambda c: send_on(0, c, made[2]), settle])
 
     def one_pass(iteration, carry):
         more = iteration < ITERS - 1
@@ -855,7 +854,7 @@
             dma((2, 1)),
             dma((2, PARTS)),
             dma((2, owners, PARTS, 2)),
-            dma((2, ITERS, 2, planes // EDGE + CHUNKS)),
+            dma((2, ITERS, 2, planes // 2 + CHUNKS)),
             dma((2, ITERS + 1, CHUNKS, 9)),
             dma((2, ITERS, CHUNKS)),
             dma((2, ITERS, CHUNKS, 3)),
@@ -889,10 +888,10 @@
         and views == 4
         and owners % 2 == 0
         and planes % views == 0
-        and planes % (EDGE * PARTS) == 0
+        and planes % (2 * PARTS) == 0
         and rim <= planes
         and columns // owners % 8 == 0
-        and lines % (GROUP * CHUNKS) == 0
+        and lines % (8 * CHUNKS) == 0
     )
     body = joint if fits else local
     return body(estimate, axial_views, lateral_views, psf_axial, psf_lateral, coverage)

time: 153 us -> 148 us (0.967)
  Pallas kernels: 146 us -> 141 us
    pallas_call x1, Pallas kernels: 146 us -> 141 us  [joint(): pl.pallas_call(functools.partial(joint_kernel, owners, views, planes, lin...]
where the time goes in v8:
time: 148 us
  Pallas kernels  141 us (95%)
  local copies, waits for them, and re-layouts  6.42 us (4%)
    pallas_call x1, Pallas kernels, joint(): pl.pallas_call(functools.partial(joint_kernel, owners, views, planes, lin...  141 us
    unnamed x13, local copies, waits for them, and re-layouts  5.95 us

profile of v8, /device:TPU:0, one launch (start us, length us, event | category | flops | bytes accessed | tf_op | source)
XLA Modules:
  0.0 148.0 jit_solution(10936623321102088981)
XLA Ops:
  0.0 0.0 copy-start.3
  0.0 0.7 copy-done.3
  0.7 0.0 copy-start.4
  0.7 0.0 copy-start.5
  0.7 0.1 copy.7
  0.8 0.6 copy-done.4
  1.4 0.0 copy-done.5
  1.4 0.1 fusion
  1.5 0.1 select_n.23
  1.6 0.1 div.11
  1.6 0.1 div.12
  1.7 0.1 broadcast_in_dim.4
  1.8 0.1 reshape.20.cover_ref
  1.9 0.0 copy-start
  1.9 1.2 copy-done
  3.1 0.0 copy-start.1
  3.1 1.2 copy-done.1
  4.4 0.0 copy-start.2
  4.4 1.2 copy-done.2
  5.6 141.4 %shard_map.64 = f32[2,2,4,128,128]{4,3,2,1,0:T(8,128)S(1)} custom-call(f32[99]{0:T(128)S(1)} %div.13.psf_ref, f32[2,2,4,128,128]{4,3,2,1,0:T(8,128)S(1)} %bitcast.9, f32[16,128,128]{2,1,0:T(8,128)S(1)} %bitcast.10, f32[16,128,128]{2,1,0:T(8,128)S(1)} %bitcast.11, f32[8,128]{1,0:T(8,128)S(1)} %reshape.20.cover_ref), custom_call_target="tpu_custom_call" | custom-call | tf_op jit(solution)/shard_map/pallas_call | solution.py:829
  147.0 1.0 copy.9
  (2 shorter events, 0.0 us)
Async XLA Ops:
  0.0 0.7 copy-start.3
  0.7 0.7 copy-start.4
  0.7 0.7 copy-start.5
  1.9 1.2 copy-start
  3.1 1.2 copy-start.1
  4.4 1.2 copy-start.2
